TPU v7x, 512 devices: a whole 4x8x8 slice. The times are simulated.
512 devices in a mesh: stretch: 8 (over z_lo, core), seq: 64 (over z_hi, x, y).
Axes of the slice: x: 4, y: 8, z: 8 (z_hi: 2, z_lo: 4; z = z_hi * 4 + z_lo), core: 2. Of those that a mesh axis runs over, the one named last changes fastest.
Arguments:
- query: bfloat16 [8, 2048, 4096], P('stretch', 'seq'), may hold values from -120 to 120
- keys: bfloat16 [8, 2048, 4096], P('stretch', 'seq'), may hold values from -4 to 4
- values: bfloat16 [8, 2048, 4096], P('stretch', 'seq'), may hold values from -6 to 6
- text_keys: bfloat16 [8, 64, 128, 256], P('stretch', 'seq'), may hold values from -6 to 6
- text_values: bfloat16 [8, 64, 128, 256], P('stretch', 'seq'), may hold values from -6 to 6
- caption_len: int32 [8, 4], P('stretch'), may hold values from 1 to 128, as said below
- noise_level: int32 [8, 4], P('stretch'), may hold values from 0 to 31, as said below
- gate_table: bfloat16 [32, 4096], replicated, may hold values from 0.099609375 to 1.8984375
Outputs:
- mixed: bfloat16 [8, 2048, 4096], P('stretch', 'seq')
Inputs may be any that keep to these rules, and one draw needn't show every extreme that they name: `caption_len`: some stretch of some video has all 128 caption tokens. `noise_level`: levels rise with the stretch: stretch c of every video has a level from c * (4) to (c + 1) * 4 - 1, except that stretch 8 - 1 of video 0 has level 31.
All inputs are finite; a program needn't handle non-finite values.
Results may differ from a plain program's by a relative error of at most 0.0056.
Values may be sent and summed in bfloat16 or wider, within the bound.
No kernel may reach another device: no remote copies, remote signals or barrier semaphores. Data moves between devices by JAX's collectives and lax.ppermute only.
A program may use at most 64 MiB of HBM per device.

v0:
```python
import math

import jax
import jax.numpy as jnp
from jax import lax
from jax.sharding import PartitionSpec as P

HD = 128
SPAN = 16


def partner(shard, axis, distance):
    return lax.ppermute(shard, axis, [(i, i ^ 1 << distance) for i in range(lax.axis_size(axis))])


def shifted(block, axis, distance):
    devices = range(lax.axis_size(axis))
    route = [(i - distance, i) for i in devices if i - distance in devices]
    return lax.ppermute(block, axis, route)


def regroup(blocks, seq_index, going_back):
    tok_rows, layers, group_size, group_width = blocks.shape
    for bit_index in range(group_size.bit_length() - 1):
        view = blocks.reshape(
            tok_rows, layers, group_size // (2 << bit_index), 2, 1 << bit_index, group_width
        )
        lower = view[:, :, :, 0]
        higher = view[:, :, :, 1]
        upper_half = seq_index >> bit_index & 1 == 1
        outgoing = jnp.where(upper_half, lower, higher)
        if going_back:
            arrived = partner(outgoing, "seq", bit_index)
        else:
            arrived = partner(outgoing, "seq", bit_index)
        new_lower = jnp.where(upper_half, arrived, lower)
        new_higher = jnp.where(upper_half, higher, arrived)
        blocks = jnp.stack([new_lower, new_higher], axis=3).reshape(
            tok_rows, layers, group_size, group_width
        )
    return blocks


def attend_heads(
    query_rows, own_keys, own_values, prior_keys, prior_values, text_k, text_v, prior_flag, caption
):
    rows = query_rows.shape[0]
    count = query_rows.shape[1] // HD
    block_rows = 512
    block_count = rows // block_rows
    key_mask = jnp.concatenate(
        [
            jnp.ones((rows,), bool),
            jnp.full((rows,), prior_flag),
            jnp.arange(text_k.shape[0], dtype=jnp.int32) < caption,
        ]
    )
    factor = 1.0 / math.sqrt(HD)

    def one_head(head):
        start = head * HD

        def columns(array):
            return lax.dynamic_slice_in_dim(array, start, HD, 1)

        all_keys = jnp.concatenate(
            [columns(own_keys), columns(prior_keys), columns(text_k)], axis=0
        )
        all_values = jnp.concatenate(
            [columns(own_values), columns(prior_values), columns(text_v)], axis=0
        )
        query_blocks = columns(query_rows).reshape(block_count, block_rows, HD)

        def one_block(block_query):
            scores = (
                lax.dot_general(
                    block_query,
                    all_keys,
                    (((1,), (1,)), ((), ())),
                    preferred_element_type=jnp.float32,
                )
                * factor
            )
            scores = jnp.where(key_mask[None, :], scores, -1e30)
            row_max = jnp.max(scores, axis=1, keepdims=True)
            weights = jnp.exp(scores - row_max)
            total = jnp.sum(weights, axis=1, keepdims=True)
            weights_b = weights.astype(jnp.bfloat16)
            result = jnp.dot(weights_b, all_values, preferred_element_type=jnp.float32) / total
            return result.astype(jnp.bfloat16)

        return lax.map(one_block, query_blocks).reshape(rows, HD)

    outputs = lax.map(one_head, jnp.arange(count))
    return jnp.moveaxis(outputs, 0, 1).reshape(rows, count * HD)


def body(query, keys, values, text_keys, text_values, caption_len, noise_level, gate_table):
    tok_rows = query.shape[1]
    width = query.shape[2]
    group_width = width // SPAN
    seq_index = lax.axis_index("seq")
    stretch_index = lax.axis_index("stretch")
    sample = seq_index // SPAN

    def split(array):
        return array[0].reshape(tok_rows, 1, SPAN, group_width)

    local = jnp.concatenate([split(query), split(keys), split(values)], axis=1)
    earlier = shifted(local[:, 1:], "stretch", 1)
    outgoing_set = jnp.concatenate([local, earlier], axis=1)
    moved = regroup(outgoing_set, seq_index, False)
    heads_view = moved[:, :3]
    prior_view = moved[:, 3:]
    rows = tok_rows * SPAN
    picked = jnp.arange(caption_len.shape[1]) == sample
    caption = jnp.sum(jnp.where(picked, caption_len[0], 0))
    level = jnp.sum(jnp.where(picked, noise_level[0], 0))
    attended = attend_heads(
        heads_view[:, 0].reshape(rows, group_width),
        heads_view[:, 1].reshape(rows, group_width),
        heads_view[:, 2].reshape(rows, group_width),
        prior_view[:, 0].reshape(rows, group_width),
        prior_view[:, 1].reshape(rows, group_width),
        text_keys[0, 0],
        text_values[0, 0],
        stretch_index > 0,
        caption,
    )
    returned = regroup(attended.reshape(tok_rows, 1, SPAN, group_width), seq_index, True)
    level_hot = (jnp.arange(gate_table.shape[0]) == level).astype(gate_table.dtype)
    gate = jnp.dot(level_hot[None, :], gate_table, preferred_element_type=jnp.float32)
    mixed = (gate * returned.reshape(tok_rows, width).astype(jnp.float32)).astype(jnp.bfloat16)
    return mixed[None]


def solution(mesh):
    placed = (
        P("stretch", "seq", None),
        P("stretch", "seq", None),
        P("stretch", "seq", None),
        P("stretch", "seq", None, None),
        P("stretch", "seq", None, None),
        P("stretch", None),
        P("stretch", None),
        P(),
    )
    return jax.shard_map(
        body, mesh=mesh, in_specs=placed, out_specs=P("stretch", "seq", None), check_vma=False
    )
```

profile of v0, /device:TPU:70, one launch (start us, length us, event | category | flops | bytes accessed | tf_op | source)
XLA Modules:
  0.0 166.2 jit_solution(6383314736842571246)
XLA Ops:
  0.0 1.1 copy.84
  1.1 1.0 copy.85
  2.2 1.9 %collective-permute-start = (bf16[32,2,16,256]{3,2,0,1:T(8,128)(2,1)S(1)}, bf16[32,2,16,256]{3,2,0,1:T(8,128)(2,1)S(1)}, u32[]{:S(2)}, u32[]{:S(2)}) collective-permute-start(bf16[32,2,16,256]{3,2,0,1:T(8,128)(2,1)S(1)} %pad_maximum_fusion.5), channel_id=1, source_target_pairs={{0,64},{64,128},{128,192},{192,256},{256,320},{320,384},{384,448},... | collective-permute-start | bytes 1572872 | tf_op jit(solution)/shard_map/ppermute | solution.py:19
  4.1 0.2 concatenate.30
  4.3 0.2 concatenate.31
  4.5 0.2 concatenate.29
  4.7 0.1 copy.54
  4.8 0.1 copy.55
  4.9 0.1 copy.56
  5.0 7.7 %collective-permute-done = bf16[32,2,16,256]{3,2,0,1:T(8,128)(2,1)S(1)} collective-permute-done((bf16[32,2,16,256]{3,2,0,1:T(8,128)(2,1)S(1)}, bf16[32,2,16,256]{3,2,0,1:T(8,128)(2,1)S(1)}, u32[]{:S(2)}, u32[]{:S(2)}) %collective-permute-start) | collective-permute-done | bytes 524320 | tf_op jit(solution)/shard_map/ppermute | solution.py:19
  12.7 0.2 copy.53
  12.9 0.2 pad_maximum_fusion
  13.1 0.4 copy.105
  13.5 0.1 broadcast_select_fusion.2
  13.6 3.5 %collective-permute-start.1 = (bf16[32,5,8,1,256]{4,0,2,1,3:T(8,128)(2,1)S(1)}, bf16[32,5,8,1,256]{4,0,2,1,3:T(8,128)(2,1)S(1)}, u32[]{:S(2)}, u32[]{:S(2)}) collective-permute-start(bf16[32,5,8,1,256]{4,0,2,1,3:T(8,128)(2,1)S(1)} %broadcast_select_fusion.2), channel_id=1, source_target_pairs={{0,1},{1,0},{2,3},{3,2},{4,5},{5,4},{6,7},{7,6},{8,9},{9,8},{10,11... | collective-permute-start | bytes 1966088 | tf_op jit(solution)/shard_map/ppermute | solution.py:13
  17.1 15.0 %collective-permute-done.1 = bf16[32,5,8,1,256]{4,0,2,1,3:T(8,128)(2,1)S(1)} collective-permute-done((bf16[32,5,8,1,256]{4,0,2,1,3:T(8,128)(2,1)S(1)}, bf16[32,5,8,1,256]{4,0,2,1,3:T(8,128)(2,1)S(1)}, u32[]{:S(2)}, u32[]{:S(2)}) %collective-permute-start.1) | collective-permute-done | bytes 655392 | tf_op jit(solution)/shard_map/ppermute | solution.py:13
  32.1 0.2 broadcast_select_fusion
  32.3 0.1 pad_maximum_fusion.4
  32.4 0.1 broadcast_select_fusion.3
  32.5 4.5 %collective-permute-start.2 = (bf16[32,5,4,2,256]{4,0,3,2,1:T(8,128)(2,1)S(1)}, bf16[32,5,4,2,256]{4,0,3,2,1:T(8,128)(2,1)S(1)}, u32[]{:S(2)}, u32[]{:S(2)}) collective-permute-start(bf16[32,5,4,2,256]{4,0,3,2,1:T(8,128)(2,1)S(1)} %broadcast_select_fusion.3), channel_id=1, source_target_pairs={{0,2},{1,3},{2,0},{3,1},{4,6},{5,7},{6,4},{7,5},{8,10},{9,11},{10,... | collective-permute-start | bytes 1966088 | tf_op jit(solution)/shard_map/ppermute | solution.py:13
  37.0 28.1 %collective-permute-done.2 = bf16[32,5,4,2,256]{4,0,3,2,1:T(8,128)(2,1)S(1)} collective-permute-done((bf16[32,5,4,2,256]{4,0,3,2,1:T(8,128)(2,1)S(1)}, bf16[32,5,4,2,256]{4,0,3,2,1:T(8,128)(2,1)S(1)}, u32[]{:S(2)}, u32[]{:S(2)}) %collective-permute-start.2) | collective-permute-done | bytes 655392 | tf_op jit(solution)/shard_map/ppermute | solution.py:13
  65.2 0.1 select_bitcast_fusion.5
  65.3 0.1 pad_maximum_fusion.1
  65.4 0.1 copy.62
  65.5 0.1 broadcast_select_fusion.4
  65.6 7.7 %collective-permute-start.3 = (bf16[32,5,2,4,256]{4,0,3,2,1:T(8,128)(2,1)S(1)}, bf16[32,5,2,4,256]{4,0,3,2,1:T(8,128)(2,1)S(1)}, u32[]{:S(2)}, u32[]{:S(2)}) collective-permute-start(bf16[32,5,2,4,256]{4,0,3,2,1:T(8,128)(2,1)S(1)} %broadcast_select_fusion.4), channel_id=1, source_target_pairs={{0,4},{1,5},{2,6},{3,7},{4,0},{5,1},{6,2},{7,3},{8,12},{9,13},{10,... | collective-permute-start | bytes 1966088 | tf_op jit(solution)/shard_map/ppermute | solution.py:13
  73.3 29.1 %collective-permute-done.3 = bf16[32,5,2,4,256]{4,0,3,2,1:T(8,128)(2,1)S(1)} collective-permute-done((bf16[32,5,2,4,256]{4,0,3,2,1:T(8,128)(2,1)S(1)}, bf16[32,5,2,4,256]{4,0,3,2,1:T(8,128)(2,1)S(1)}, u32[]{:S(2)}, u32[]{:S(2)}) %collective-permute-start.3) | collective-permute-done | bytes 655392 | tf_op jit(solution)/shard_map/ppermute | solution.py:13
  102.4 0.1 select_bitcast_fusion.3
  102.5 0.1 pad_maximum_fusion.2
  102.7 0.1 copy.64
  102.8 0.1 broadcast_select_fusion.5
  102.9 2.7 %collective-permute-start.4 = (bf16[32,5,1,8,256]{4,0,3,1,2:T(8,128)(2,1)S(1)}, bf16[32,5,1,8,256]{4,0,3,1,2:T(8,128)(2,1)S(1)}, u32[]{:S(2)}, u32[]{:S(2)}) collective-permute-start(bf16[32,5,1,8,256]{4,0,3,1,2:T(8,128)(2,1)S(1)} %broadcast_select_fusion.5), channel_id=1, source_target_pairs={{0,8},{1,9},{2,10},{3,11},{4,12},{5,13},{6,14},{7,15},{8,0},{9,1},... | collective-permute-start | bytes 1966088 | tf_op jit(solution)/shard_map/ppermute | solution.py:13
  105.7 0.7 fusion.39
  106.4 0.6 iota_compare_fusion
  107.1 13.5 %collective-permute-done.4 = bf16[32,5,1,8,256]{4,0,3,1,2:T(8,128)(2,1)S(1)} collective-permute-done((bf16[32,5,1,8,256]{4,0,3,1,2:T(8,128)(2,1)S(1)}, bf16[32,5,1,8,256]{4,0,3,1,2:T(8,128)(2,1)S(1)}, u32[]{:S(2)}, u32[]{:S(2)}) %collective-permute-start.4) | collective-permute-done | bytes 655392 | tf_op jit(solution)/shard_map/ppermute | solution.py:13
  120.6 0.1 select_bitcast_fusion.1
  120.7 0.1 pad_maximum_fusion.3
  120.8 0.7 copy.104
  121.6 0.1 fusion.44
  121.7 0.7 copy-done.3
  122.5 6.2 %while.10 = (s32[]{:T(128)}, bf16[2,512,128]{2,1,0:T(8,128)(2,1)S(1)}, pred[1152]{0:T(1024)(128)(4,1)S(1)}, s32[2]{0:T(128)S(1)}, bf16[512,256]{1,0:T(8,128)(2,1...) while((s32[]{:T(128)}, ...), condition=%wide.region_5.6_spmd, body=%wide.region_2.5_spmd.sunk | while | flops 308018176 | bytes 9122011 | solution.py:94
  122.5 0.6 dynamic_slice.47
  123.8 0.6 fusion.54
  124.4 0.5 fusion.55
  125.0 0.6 fusion.56
  125.6 0.7 dynamic_slice.47
  126.9 0.6 fusion.54
  127.5 0.5 fusion.55
  128.1 0.6 fusion.56
  128.7 0.3 copy.67
  129.0 0.2 reshape_reshape_reshape.3
  129.2 0.4 fusion.45
  129.6 1.9 %collective-permute-start.5 = (bf16[32,1,8,1,256]{4,2,0,3,1:T(8,128)(2,1)S(1)}, bf16[32,1,8,1,256]{4,2,0,3,1:T(8,128)(2,1)S(1)}, u32[]{:S(2)}, u32[]{:S(2)}) collective-permute-start(bf16[32,1,8,1,256]{4,2,0,3,1:T(8,128)(2,1)S(1)} %bitcast_select_fusion.1), channel_id=1, source_target_pairs={{0,1},{1,0},{2,3},{3,2},{4,5},{5,4},{6,7},{7,6},{8,9},{9,8},{10,11... | collective-permute-start | bytes 393224 | tf_op jit(solution)/shard_map/ppermute | solution.py:13
  131.5 4.9 %collective-permute-done.5 = bf16[32,1,8,1,256]{4,2,0,3,1:T(8,128)(2,1)S(1)} collective-permute-done((bf16[32,1,8,1,256]{4,2,0,3,1:T(8,128)(2,1)S(1)}, bf16[32,1,8,1,256]{4,2,0,3,1:T(8,128)(2,1)S(1)}, u32[]{:S(2)}, u32[]{:S(2)}) %collective-permute-start.5) | collective-permute-done | bytes 131104 | tf_op jit(solution)/shard_map/ppermute | solution.py:13
  136.6 3.5 %collective-permute-start.6 = (bf16[32,1,4,2,256]{4,0,2,3,1:T(8,128)(2,1)S(1)}, bf16[32,1,4,2,256]{4,0,2,3,1:T(8,128)(2,1)S(1)}, u32[]{:S(2)}, u32[]{:S(2)}) collective-permute-start(bf16[32,1,4,2,256]{4,0,2,3,1:T(8,128)(2,1)S(1)} %broadcast_select_fusion.6), channel_id=1, source_target_pairs={{0,2},{1,3},{2,0},{3,1},{4,6},{5,7},{6,4},{7,5},{8,10},{9,11},{10,... | collective-permute-start | bytes 393224 | tf_op jit(solution)/shard_map/ppermute | solution.py:13
  140.0 5.7 %collective-permute-done.6 = bf16[32,1,4,2,256]{4,0,2,3,1:T(8,128)(2,1)S(1)} collective-permute-done((bf16[32,1,4,2,256]{4,0,2,3,1:T(8,128)(2,1)S(1)}, bf16[32,1,4,2,256]{4,0,2,3,1:T(8,128)(2,1)S(1)}, u32[]{:S(2)}, u32[]{:S(2)}) %collective-permute-start.6) | collective-permute-done | bytes 131104 | tf_op jit(solution)/shard_map/ppermute | solution.py:13
  145.9 4.5 %collective-permute-start.7 = (bf16[32,1,2,4,256]{4,0,3,2,1:T(8,128)(2,1)S(1)}, bf16[32,1,2,4,256]{4,0,3,2,1:T(8,128)(2,1)S(1)}, u32[]{:S(2)}, u32[]{:S(2)}) collective-permute-start(bf16[32,1,2,4,256]{4,0,3,2,1:T(8,128)(2,1)S(1)} %broadcast_select_fusion.7), channel_id=1, source_target_pairs={{0,4},{1,5},{2,6},{3,7},{4,0},{5,1},{6,2},{7,3},{8,12},{9,13},{10,... | collective-permute-start | bytes 393224 | tf_op jit(solution)/shard_map/ppermute | solution.py:13
  150.3 7.7 %collective-permute-done.7 = bf16[32,1,2,4,256]{4,0,3,2,1:T(8,128)(2,1)S(1)} collective-permute-done((bf16[32,1,2,4,256]{4,0,3,2,1:T(8,128)(2,1)S(1)}, bf16[32,1,2,4,256]{4,0,3,2,1:T(8,128)(2,1)S(1)}, u32[]{:S(2)}, u32[]{:S(2)}) %collective-permute-start.7) | collective-permute-done | bytes 131104 | tf_op jit(solution)/shard_map/ppermute | solution.py:13
  158.2 2.7 %collective-permute-start.8 = (bf16[32,1,1,8,256]{4,0,3,2,1:T(8,128)(2,1)S(1)}, bf16[32,1,1,8,256]{4,0,3,2,1:T(8,128)(2,1)S(1)}, u32[]{:S(2)}, u32[]{:S(2)}) collective-permute-start(bf16[32,1,1,8,256]{4,0,3,2,1:T(8,128)(2,1)S(1)} %broadcast_select_fusion.8), channel_id=1, source_target_pairs={{0,8},{1,9},{2,10},{3,11},{4,12},{5,13},{6,14},{7,15},{8,0},{9,1},... | collective-permute-start | bytes 393224 | tf_op jit(solution)/shard_map/ppermute | solution.py:13
  160.9 0.8 fusion.36
  161.7 3.3 %collective-permute-done.8 = bf16[32,1,1,8,256]{4,0,3,2,1:T(8,128)(2,1)S(1)} collective-permute-done((bf16[32,1,1,8,256]{4,0,3,2,1:T(8,128)(2,1)S(1)}, bf16[32,1,1,8,256]{4,0,3,2,1:T(8,128)(2,1)S(1)}, u32[]{:S(2)}, u32[]{:S(2)}) %collective-permute-start.8) | collective-permute-done | bytes 131104 | tf_op jit(solution)/shard_map/ppermute | solution.py:13
  165.1 0.3 copy.74
  165.4 0.1 reshape.192
  165.5 0.7 multiply_convert_fusion
  (43 shorter events, 0.7 us)
Async XLA Ops:
  0.0 160.9 %copy-start = (bf16[32,4096]{1,0:T(8,128)(2,1)S(1)}, bf16[32,4096]{1,0:T(8,128)(2,1)}, u32[]{:S(2)}) copy-start(bf16[32,4096]{1,0:T(8,128)(2,1)} %param.17) | copy-start | bytes 786436
  0.0 4.1 %copy-start.1 = (bf16[1,32,4096]{2,1,0:T(8,128)(2,1)S(1)}, bf16[1,32,4096]{2,1,0:T(8,128)(2,1)}, u32[]{:S(2)}) copy-start(bf16[1,32,4096]{2,1,0:T(8,128)(2,1)} %param.11) | copy-start | bytes 786436
  0.0 4.3 %copy-start.2 = (bf16[1,32,4096]{2,1,0:T(8,128)(2,1)S(1)}, bf16[1,32,4096]{2,1,0:T(8,128)(2,1)}, u32[]{:S(2)}) copy-start(bf16[1,32,4096]{2,1,0:T(8,128)(2,1)} %param.12) | copy-start | bytes 786436
  1.1 3.4 %copy-start.5 = (bf16[1,32,4096]{2,1,0:T(8,128)(2,1)S(1)}, bf16[1,32,4096]{2,1,0:T(8,128)(2,1)}, u32[]{:S(2)}) copy-start(bf16[1,32,4096]{2,1,0:T(8,128)(2,1)} %param.10) | copy-start | bytes 786436
  2.2 10.5 %collective-permute-start = (bf16[32,2,16,256]{3,2,0,1:T(8,128)(2,1)S(1)}, bf16[32,2,16,256]{3,2,0,1:T(8,128)(2,1)S(1)}, u32[]{:S(2)}, u32[]{:S(2)}) collective-permute-start(bf16[32,2,16,256]{3,2,0,1:T(8,128)(2,1)S(1)} %pad_maximum_fusion.5), channel_id=1, source_target_pairs={{0,64},{64,128},{128,192},{192,256},{256,320},{320,384},{384,448},... | collective-permute-start | bytes 1572872 | tf_op jit(solution)/shard_map/ppermute | solution.py:19
  13.6 18.5 %collective-permute-start.1 = (bf16[32,5,8,1,256]{4,0,2,1,3:T(8,128)(2,1)S(1)}, bf16[32,5,8,1,256]{4,0,2,1,3:T(8,128)(2,1)S(1)}, u32[]{:S(2)}, u32[]{:S(2)}) collective-permute-start(bf16[32,5,8,1,256]{4,0,2,1,3:T(8,128)(2,1)S(1)} %broadcast_select_fusion.2), channel_id=1, source_target_pairs={{0,1},{1,0},{2,3},{3,2},{4,5},{5,4},{6,7},{7,6},{8,9},{9,8},{10,11... | collective-permute-start | bytes 1966088 | tf_op jit(solution)/shard_map/ppermute | solution.py:13
  32.5 32.6 %collective-permute-start.2 = (bf16[32,5,4,2,256]{4,0,3,2,1:T(8,128)(2,1)S(1)}, bf16[32,5,4,2,256]{4,0,3,2,1:T(8,128)(2,1)S(1)}, u32[]{:S(2)}, u32[]{:S(2)}) collective-permute-start(bf16[32,5,4,2,256]{4,0,3,2,1:T(8,128)(2,1)S(1)} %broadcast_select_fusion.3), channel_id=1, source_target_pairs={{0,2},{1,3},{2,0},{3,1},{4,6},{5,7},{6,4},{7,5},{8,10},{9,11},{10,... | collective-permute-start | bytes 1966088 | tf_op jit(solution)/shard_map/ppermute | solution.py:13
  65.6 36.8 %collective-permute-start.3 = (bf16[32,5,2,4,256]{4,0,3,2,1:T(8,128)(2,1)S(1)}, bf16[32,5,2,4,256]{4,0,3,2,1:T(8,128)(2,1)S(1)}, u32[]{:S(2)}, u32[]{:S(2)}) collective-permute-start(bf16[32,5,2,4,256]{4,0,3,2,1:T(8,128)(2,1)S(1)} %broadcast_select_fusion.4), channel_id=1, source_target_pairs={{0,4},{1,5},{2,6},{3,7},{4,0},{5,1},{6,2},{7,3},{8,12},{9,13},{10,... | collective-permute-start | bytes 1966088 | tf_op jit(solution)/shard_map/ppermute | solution.py:13
  102.8 2.9 %copy-start.6 = (s32[1,4]{1,0:T(1,128)S(1)}, s32[1,4]{1,0:T(1,128)}, u32[]{:S(2)}) copy-start(s32[1,4]{1,0:T(1,128)} %param.16) | copy-start | bytes 52
  102.8 2.9 %copy-start.7 = (s32[1,4]{1,0:T(1,128)S(1)}, s32[1,4]{1,0:T(1,128)}, u32[]{:S(2)}) copy-start(s32[1,4]{1,0:T(1,128)} %param.15) | copy-start | bytes 52
  102.9 17.7 %collective-permute-start.4 = (bf16[32,5,1,8,256]{4,0,3,1,2:T(8,128)(2,1)S(1)}, bf16[32,5,1,8,256]{4,0,3,1,2:T(8,128)(2,1)S(1)}, u32[]{:S(2)}, u32[]{:S(2)}) collective-permute-start(bf16[32,5,1,8,256]{4,0,3,1,2:T(8,128)(2,1)S(1)} %broadcast_select_fusion.5), channel_id=1, source_target_pairs={{0,8},{1,9},{2,10},{3,11},{4,12},{5,13},{6,14},{7,15},{8,0},{9,1},... | collective-permute-start | bytes 1966088 | tf_op jit(solution)/shard_map/ppermute | solution.py:13
  121.6 0.8 copy-start.3
  121.6 0.9 copy-start.4
  129.6 6.9 %collective-permute-start.5 = (bf16[32,1,8,1,256]{4,2,0,3,1:T(8,128)(2,1)S(1)}, bf16[32,1,8,1,256]{4,2,0,3,1:T(8,128)(2,1)S(1)}, u32[]{:S(2)}, u32[]{:S(2)}) collective-permute-start(bf16[32,1,8,1,256]{4,2,0,3,1:T(8,128)(2,1)S(1)} %bitcast_select_fusion.1), channel_id=1, source_target_pairs={{0,1},{1,0},{2,3},{3,2},{4,5},{5,4},{6,7},{7,6},{8,9},{9,8},{10,11... | collective-permute-start | bytes 393224 | tf_op jit(solution)/shard_map/ppermute | solution.py:13
  136.6 9.2 %collective-permute-start.6 = (bf16[32,1,4,2,256]{4,0,2,3,1:T(8,128)(2,1)S(1)}, bf16[32,1,4,2,256]{4,0,2,3,1:T(8,128)(2,1)S(1)}, u32[]{:S(2)}, u32[]{:S(2)}) collective-permute-start(bf16[32,1,4,2,256]{4,0,2,3,1:T(8,128)(2,1)S(1)} %broadcast_select_fusion.6), channel_id=1, source_target_pairs={{0,2},{1,3},{2,0},{3,1},{4,6},{5,7},{6,4},{7,5},{8,10},{9,11},{10,... | collective-permute-start | bytes 393224 | tf_op jit(solution)/shard_map/ppermute | solution.py:13
  145.9 12.2 %collective-permute-start.7 = (bf16[32,1,2,4,256]{4,0,3,2,1:T(8,128)(2,1)S(1)}, bf16[32,1,2,4,256]{4,0,3,2,1:T(8,128)(2,1)S(1)}, u32[]{:S(2)}, u32[]{:S(2)}) collective-permute-start(bf16[32,1,2,4,256]{4,0,3,2,1:T(8,128)(2,1)S(1)} %broadcast_select_fusion.7), channel_id=1, source_target_pairs={{0,4},{1,5},{2,6},{3,7},{4,0},{5,1},{6,2},{7,3},{8,12},{9,13},{10,... | collective-permute-start | bytes 393224 | tf_op jit(solution)/shard_map/ppermute | solution.py:13
  158.2 6.9 %collective-permute-start.8 = (bf16[32,1,1,8,256]{4,0,3,2,1:T(8,128)(2,1)S(1)}, bf16[32,1,1,8,256]{4,0,3,2,1:T(8,128)(2,1)S(1)}, u32[]{:S(2)}, u32[]{:S(2)}) collective-permute-start(bf16[32,1,1,8,256]{4,0,3,2,1:T(8,128)(2,1)S(1)} %broadcast_select_fusion.8), channel_id=1, source_target_pairs={{0,8},{1,9},{2,10},{3,11},{4,12},{5,13},{6,14},{7,15},{8,0},{9,1},... | collective-permute-start | bytes 393224 | tf_op jit(solution)/shard_map/ppermute | solution.py:13
where the time goes:
time: 167 us; the launch traced here: 166 us
  waiting for transfers between devices  115 us (69%)
  starting transfers between devices  32.9 us (20%)
  local copies, waits for them, and re-layouts  8.05 us (5%)
  other arithmetic  5 us (3%)
  matrix products  3.16 us (2%)
    ppermute x8, waiting for transfers between devices, partner(): lax.ppermute(shard, axis, [(i, i ^ 1 << distance) for i in range(lax.axis...  107 us
    ppermute x8, starting transfers between devices, partner(): lax.ppermute(shard, axis, [(i, i ^ 1 << distance) for i in range(lax.axis...  31 us
    ppermute x1, waiting for transfers between devices, shifted(): return lax.ppermute(block, axis, route)  7.72 us
  transfers between devices with their start and end apart: 9, of which 9 were waited for; matrix products, arithmetic and copies ran while one was open for 2% of the time, Pallas kernels for 0%

commit v1 on v0

v1 whole, which is shorter than its diff:
```python
import math

import jax
import jax.numpy as jnp
from jax import lax
from jax.experimental import pallas as pl
from jax.experimental.pallas import tpu as pltpu
from jax.sharding import PartitionSpec as P

HD = 128
SPAN = 16
BLOCK_ROWS = 256
SCALE = math.log2(math.e) / math.sqrt(HD)
NT = (((1,), (1,)), ((), ()))


def attend_kernel(info_ref, q_ref, k_ref, v_ref, kp_ref, vp_ref, tk_ref, tv_ref, gate_ref, out_ref):
    rows, width = q_ref.shape
    caption = info_ref[0]
    has_prior = info_ref[1] > 0
    usable = lax.broadcasted_iota(jnp.int32, (1, tk_ref.shape[0]), 1) < caption
    for head in range(width // HD):
        cols = slice(head * HD, (head + 1) * HD)
        for block in range(rows // BLOCK_ROWS):
            span = slice(block * BLOCK_ROWS, (block + 1) * BLOCK_ROWS)
            query = q_ref[span, cols]

            def scores(keys_ref):
                return lax.dot_general(query, keys_ref[:, cols], NT, preferred_element_type=jnp.float32)

            own, prior, text = scores(k_ref), scores(kp_ref), scores(tk_ref)
            text = jnp.where(usable, text, -1e30)
            row_max = jnp.maximum(
                jnp.max(own, axis=1, keepdims=True), jnp.max(text, axis=1, keepdims=True)
            )
            with_prior = jnp.maximum(row_max, jnp.max(prior, axis=1, keepdims=True))
            row_max = jnp.where(has_prior, with_prior, row_max)
            prior_max = jnp.where(has_prior, row_max, 1e30)
            own = jnp.exp2((own - row_max) * SCALE)
            prior = jnp.exp2((prior - prior_max) * SCALE)
            text = jnp.exp2((text - row_max) * SCALE)
            total = (
                jnp.sum(own, axis=1, keepdims=True)
                + jnp.sum(prior, axis=1, keepdims=True)
                + jnp.sum(text, axis=1, keepdims=True)
            )

            def weighted(weights, values_ref):
                return jnp.dot(
                    weights.astype(jnp.bfloat16), values_ref[:, cols], preferred_element_type=jnp.float32
                )

            result = weighted(own, v_ref) + weighted(prior, vp_ref) + weighted(text, tv_ref)
            attended = (result / total).astype(jnp.bfloat16).astype(jnp.float32)
            gated = gate_ref[:, cols].astype(jnp.float32) * attended
            out_ref[span, cols] = gated.astype(jnp.bfloat16)


def attend(info, *arrays):
    vmem = pl.BlockSpec(memory_space=pltpu.VMEM)
    return pl.pallas_call(
        attend_kernel,
        out_shape=jax.ShapeDtypeStruct(arrays[0].shape, jnp.bfloat16),
        in_specs=[pl.BlockSpec(memory_space=pltpu.SMEM)] + [vmem] * len(arrays),
        out_specs=vmem,
        compiler_params=pltpu.CompilerParams(vmem_limit_bytes=32 * 1024 * 1024),
        cost_estimate=pl.CostEstimate(flops=604_000_000, bytes_accessed=2_000_000, transcendentals=1_200_000),
    )(info, *arrays)


def swap(blocks):
    videos = lax.axis_size("seq") // SPAN
    groups = [[video * SPAN + i for i in range(SPAN)] for video in range(videos)]
    return lax.all_to_all(blocks, "seq", 0, 0, axis_index_groups=groups)


def body(query, keys, values, text_keys, text_values, caption_len, noise_level, gate_table):
    tok_rows, width = query.shape[1:]
    group_width = width // SPAN
    rows = tok_rows * SPAN
    seq_index = lax.axis_index("seq")
    stretch_index = lax.axis_index("stretch")
    sample = seq_index // SPAN
    group = seq_index % SPAN

    def split(array):
        return array[0].reshape(tok_rows, SPAN, group_width).transpose(1, 0, 2)

    moved = swap(jnp.stack([split(query), split(keys), split(values)], axis=1))
    own = moved.transpose(1, 0, 2, 3).reshape(3, rows, group_width)
    last = lax.axis_size("stretch") - 1
    prior = lax.ppermute(own[1:], "stretch", [(i, i + 1) for i in range(last)])

    caption = lax.dynamic_index_in_dim(caption_len[0], sample, 0, False)
    level = lax.dynamic_index_in_dim(noise_level[0], sample, 0, False)
    info = jnp.stack([caption, stretch_index]).astype(jnp.int32)
    gate = lax.dynamic_slice(gate_table, (level, group * group_width), (1, group_width))
    mixed = attend(
        info, own[0], own[1], own[2], prior[0], prior[1], text_keys[0, 0], text_values[0, 0], gate
    )
    returned = swap(mixed.reshape(SPAN, tok_rows, group_width))
    return returned.transpose(1, 0, 2).reshape(1, tok_rows, width)


def solution(mesh):
    placed = (
        P("stretch", "seq", None),
        P("stretch", "seq", None),
        P("stretch", "seq", None),
        P("stretch", "seq", None, None),
        P("stretch", "seq", None, None),
        P("stretch", None),
        P("stretch", None),
        P(),
    )
    return jax.shard_map(
        body, mesh=mesh, in_specs=placed, out_specs=P("stretch", "seq", None), check_vma=False
    )
```

time: 167 us -> 61.8 us (0.37)
  the two profiles are of different devices: /device:TPU:70 before, /device:TPU:72 now
where the time goes in v1:
time: 61.8 us; the launch traced here: 61.4 us
  blocking collectives  44.1 us (71%)
  local copies, waits for them, and re-layouts  5.48 us (9%)
  waiting for transfers between devices  3.78 us (6%)
  Pallas kernels  3.22 us (5%)
  between operations  2.07 us (3%)
  starting transfers between devices  1.92 us (3%)
  other arithmetic  0.79 us (1%)
    all_to_all x2, blocking collectives, swap(): return lax.all_to_all(blocks, 'seq', 0, 0, axis_index_groups=groups)  44.1 us
    ppermute x1, waiting for transfers between devices, body(): prior = lax.ppermute(own[1:], 'stretch', [(i, i + 1) for i in range(last)])  3.78 us
    pallas_call x1, Pallas kernels, attend(): pl.pallas_call(attend_kernel, out_shape=jax.ShapeDtypeStruct(arrays[0].sh...  3.22 us
    unnamed x15, local copies, waits for them, and re-layouts  2.7 us
    ppermute x1, starting transfers between devices, body(): prior = lax.ppermute(own[1:], 'stretch', [(i, i + 1) for i in range(last)])  1.92 us
  transfers between devices with their start and end apart: 1, of which 1 were waited for; matrix products, arithmetic and copies ran while one was open for 4% of the time, Pallas kernels for 0%

profile of v1, /device:TPU:72, one launch (start us, length us, event | category | flops | bytes accessed | tf_op | source)
XLA Modules:
  0.0 61.4 jit_solution(17468587716448175852)
XLA Ops:
  0.0 0.0 copy-start.2
  0.0 1.0 %copy.18 = bf16[4,8,16,256]{3,2,1,0:T(8,128)(2,1)S(1)} copy(bf16[4,8,16,256]{3,1,2,0:T(8,128)(2,1)} %bitcast.50) | data formatting | bytes 524288
  1.0 0.0 copy-done.2
  1.1 0.0 copy-start.3
  1.1 0.9 %copy-done.3 = bf16[1,32,4096]{2,1,0:T(8,128)(2,1)S(1)} copy-done((bf16[1,32,4096]{2,1,0:T(8,128)(2,1)S(1)}, bf16[1,32,4096]{2,1,0:T(8,128)(2,1)}, u32[]{:S(2)}) %copy-start.3) | copy-done | bytes 262168
  2.1 0.1 pad_maximum_fusion
  2.2 0.2 copy.15
  2.4 29.8 %all_to_all.10 = bf16[16,3,32,256]{3,2,1,0:T(8,128)(2,1)S(1)} all-to-all(bf16[16,3,32,256]{3,2,1,0:T(8,128)(2,1)S(1)} %copy.15), channel_id=1, replica_groups={{0,1,2,3,4,5,6,7,8,9,10,11,12,13,14,15},{16,17,18,19,20,21,22,23,24,25,..., dimensions={0} | all-to-all | bytes 1572864 | tf_op jit(solution)/shard_map/all_to_all | solution.py:74
  32.3 1.9 %collective-permute-start = (bf16[2,512,256]{2,1,0:T(8,128)(2,1)S(1)}, bf16[2,512,256]{2,1,0:T(8,128)(2,1)S(1)}, u32[]{:S(2)}, u32[]{:S(2)}) collective-permute-start(bf16[2,512,256]{2,1,0:T(8,128)(2,1)S(1)} %bitcast.49), channel_id=1, source_target_pairs={{0,64},{64,128},{128,192},{192,256},{256,320},{320,384},{384,448},... | collective-permute-start | bytes 1572872 | tf_op jit(solution)/shard_map/ppermute | solution.py:92
  34.3 0.0 copy-start.4
  34.3 0.0 copy-start.5
  34.3 0.6 %copy-done.4 = s32[1,4]{1,0:T(1,128)S(1)} copy-done((s32[1,4]{1,0:T(1,128)S(1)}, s32[1,4]{1,0:T(1,128)}, u32[]{:S(2)}) %copy-start.4) | copy-done | bytes 40
  34.9 0.0 copy-done.5
  35.0 0.6 %constant_dynamic-slice_fusion = (s32[1,1]{1,0:T(1,128)}, s32[1,1]{1,0:T(1,128)}) fusion(s32[1,4]{1,0:T(1,128)S(1)} %copy-done.4, s32[]{:T(128)S(6)} %select_n.23, s32[1,4]{1,0:T(1,128)S(1)} %copy-done.5), kind=kLoop, calls=%fused_computation.4 | loop fusion | bytes 20 | tf_op jit(solution)/shard_map/jit(dynamic_index_in_dim)/dynamic_slice | solution.py:95
  37.5 0.8 %dynamic_slice.15.gate_ref = bf16[1,256]{1,0:T(2,128)(2,1)S(1)} dynamic-slice(bf16[32,4096]{1,0:T(8,128)(2,1)} %param.15, s32[]{:T(128)S(6)} %select_n.24, s32[]{:T(128)S(6)} %select_n.26), dynamic_slice_sizes={1,256} | dynamic-slice | bytes 1028 | tf_op jit(solution)/shard_map/dynamic_slice | solution.py:97
  38.2 0.7 %pad_add_fusion.info_ref = s32[2]{0:T(128)S(1)} fusion(s32[1]{0:T(128)} %bitcast.1, s32[1]{0:T(128)} %bitcast), kind=kLoop, calls=%fused_computation.3 | loop fusion | flops 2 | bytes 16 | tf_op jit(solution)/shard_map/stack | solution.py:96
  39.0 0.1 fusion
  39.0 0.0 copy-start
  39.0 0.0 copy-start.1
  39.0 3.8 %collective-permute-done = bf16[2,512,256]{2,1,0:T(8,128)(2,1)S(1)} collective-permute-done((bf16[2,512,256]{2,1,0:T(8,128)(2,1)S(1)}, bf16[2,512,256]{2,1,0:T(8,128)(2,1)S(1)}, u32[]{:S(2)}, u32[]{:S(2)}) %collective-permute-start) | collective-permute-done | bytes 524320 | tf_op jit(solution)/shard_map/ppermute | solution.py:92
  42.9 0.0 copy-done
  42.9 0.0 copy-done.1
  42.9 3.2 %shard_map.82 = bf16[512,256]{1,0:T(8,128)(2,1)S(1)} custom-call(s32[2]{0:T(128)S(1)} %pad_add_fusion.info_ref, bf16[512,256]{1,0:T(8,128)(2,1)S(1)} %bitcast.40, bf16[512,256]{1,0:T(8,128)(2,1)S(1)} %bitcast.39, bf16[512,256]{1,0:T(8,128)(2,1)S(1)} %bitcast.38, bf16[512,256]{1,0:T(8,128)(2,1)S(1)} %get-tuple-element.9.kp_ref, ...), custom_call_target="tpu_custom_call" | custom-call | flops 604000000 | bytes 2000000 | tf_op jit(solution)/shard_map/pallas_call | solution.py:61
  46.1 14.3 %all_to_all.11 = bf16[16,32,256]{2,1,0:T(8,128)(2,1)S(1)} all-to-all(bf16[16,32,256]{2,1,0:T(8,128)(2,1)S(1)} %bitcast.37), channel_id=1, replica_groups={{0,1,2,3,4,5,6,7,8,9,10,11,12,13,14,15},{16,17,18,19,20,21,22,23,24,25,..., dimensions={0} | all-to-all | bytes 524288 | tf_op jit(solution)/shard_map/all_to_all | solution.py:74
  60.4 0.1 copy.17
  60.6 0.8 %reshape.18 = bf16[1,32,4096]{2,1,0:T(8,128)(2,1)} reshape(bf16[32,16,256]{2,1,0:T(8,128)(2,1)S(1)} %copy.17) | data formatting | bytes 524288 | tf_op jit(solution)/shard_map/reshape | solution.py:102
  (5 shorter events, 0.2 us)
Async XLA Ops:
  0.0 1.0 %copy-start.2 = (bf16[1,32,4096]{2,1,0:T(8,128)(2,1)S(1)}, bf16[1,32,4096]{2,1,0:T(8,128)(2,1)}, u32[]{:S(2)}) copy-start(bf16[1,32,4096]{2,1,0:T(8,128)(2,1)} %param.9) | copy-start | bytes 786436
  1.1 1.0 %copy-start.3 = (bf16[1,32,4096]{2,1,0:T(8,128)(2,1)S(1)}, bf16[1,32,4096]{2,1,0:T(8,128)(2,1)}, u32[]{:S(2)}) copy-start(bf16[1,32,4096]{2,1,0:T(8,128)(2,1)} %param.10) | copy-start | bytes 786436
  32.3 10.5 %collective-permute-start = (bf16[2,512,256]{2,1,0:T(8,128)(2,1)S(1)}, bf16[2,512,256]{2,1,0:T(8,128)(2,1)S(1)}, u32[]{:S(2)}, u32[]{:S(2)}) collective-permute-start(bf16[2,512,256]{2,1,0:T(8,128)(2,1)S(1)} %bitcast.49), channel_id=1, source_target_pairs={{0,64},{64,128},{128,192},{192,256},{256,320},{320,384},{384,448},... | collective-permute-start | bytes 1572872 | tf_op jit(solution)/shard_map/ppermute | solution.py:92
  34.3 0.7 %copy-start.4 = (s32[1,4]{1,0:T(1,128)S(1)}, s32[1,4]{1,0:T(1,128)}, u32[]{:S(2)}) copy-start(s32[1,4]{1,0:T(1,128)} %param.14) | copy-start | bytes 52
  34.3 0.7 %copy-start.5 = (s32[1,4]{1,0:T(1,128)S(1)}, s32[1,4]{1,0:T(1,128)}, u32[]{:S(2)}) copy-start(s32[1,4]{1,0:T(1,128)} %param.13) | copy-start | bytes 52
  39.0 3.8 %copy-start = (bf16[1,1,128,256]{3,2,1,0:T(8,128)(2,1)S(1)}, bf16[1,1,128,256]{3,2,1,0:T(8,128)(2,1)}, u32[]{:S(2)}) copy-start(bf16[1,1,128,256]{3,2,1,0:T(8,128)(2,1)} %param.11) | copy-start | bytes 196612
  39.0 3.8 %copy-start.1 = (bf16[1,1,128,256]{3,2,1,0:T(8,128)(2,1)S(1)}, bf16[1,1,128,256]{3,2,1,0:T(8,128)(2,1)}, u32[]{:S(2)}) copy-start(bf16[1,1,128,256]{3,2,1,0:T(8,128)(2,1)} %param.12) | copy-start | bytes 196612

commit v2 on v1

v2 whole, which is shorter than its diff:
```python
import math

import jax
import jax.numpy as jnp
from jax import lax
from jax.experimental import pallas as pl
from jax.experimental.pallas import tpu as pltpu
from jax.sharding import PartitionSpec as P

HD = 128
SPAN = 16
GATE_ROWS = 16
BLOCK_ROWS = 256
SCALE = math.log2(math.e) / math.sqrt(HD)
NT = (((1,), (1,)), ((), ()))
VMEM = pl.BlockSpec(memory_space=pltpu.VMEM)
SMEM = pl.BlockSpec(memory_space=pltpu.SMEM)
HBM = pl.BlockSpec(memory_space=pltpu.HBM)
PARAMS = pltpu.CompilerParams(vmem_limit_bytes=32 * 1024 * 1024)


def split_kernel(query_ref, keys_ref, values_ref, out_ref, sems):
    rows = query_ref.shape[0]
    width = out_ref.shape[2]
    copies = []
    for part, ref in enumerate((query_ref, keys_ref, values_ref)):
        for group in range(SPAN):
            copy = pltpu.make_async_copy(
                ref.at[:, pl.ds(group * width, width)],
                out_ref.at[group, pl.ds(part * rows, rows), :],
                sems.at[part, group],
            )
            copy.start()
            copies.append(copy)
    for copy in copies:
        copy.wait()


def split(query, keys, values):
    rows, width = query.shape
    return pl.pallas_call(
        split_kernel,
        out_shape=jax.ShapeDtypeStruct((SPAN, 3 * rows, width // SPAN), query.dtype),
        in_specs=[HBM] * 3,
        out_specs=VMEM,
        scratch_shapes=[pltpu.SemaphoreType.DMA((3, SPAN))],
        compiler_params=PARAMS,
    )(*(pltpu.with_memory_space_constraint(array, pltpu.HBM) for array in (query, keys, values)))


def merge_kernel(blocks_ref, out_ref, sems):
    width = blocks_ref.shape[2]
    copies = []
    for group in range(SPAN):
        copy = pltpu.make_async_copy(
            blocks_ref.at[group], out_ref.at[:, pl.ds(group * width, width)], sems.at[group]
        )
        copy.start()
        copies.append(copy)
    for copy in copies:
        copy.wait()


def merge(blocks):
    rows, width = blocks.shape[1:]
    return pl.pallas_call(
        merge_kernel,
        out_shape=jax.ShapeDtypeStruct((rows, SPAN * width), blocks.dtype),
        in_specs=[VMEM],
        out_specs=HBM,
        scratch_shapes=[pltpu.SemaphoreType.DMA((SPAN,))],
        compiler_params=PARAMS,
    )(blocks)


def block_of(ref, block, part, rows, cols):
    count = BLOCK_ROWS // rows
    tile = ref[block * count : (block + 1) * count, part * rows : (part + 1) * rows, cols]
    return tile.reshape(BLOCK_ROWS, HD)


def whole(ref, part, rows, cols):
    return ref[:, part * rows : (part + 1) * rows, cols].reshape(ref.shape[0] * rows, HD)


def dot_keys(query, keys):
    return lax.dot_general(query, keys, NT, preferred_element_type=jnp.float32)


def dot_values(weights, values):
    return jnp.dot(weights.astype(jnp.bfloat16), values, preferred_element_type=jnp.float32)


def own_kernel(
    caption_ref, level_ref, moved_ref, text_k_ref, text_v_ref, table_ref,
    acc_ref, max_ref, total_ref, gate_ref, picked, sem,
):
    rows = moved_ref.shape[1] // 3
    width = moved_ref.shape[2]
    seq_index = lax.axis_index("seq")
    sample = seq_index // SPAN
    group = seq_index % SPAN
    level = level_ref[0, sample]
    first = pl.multiple_of(level // GATE_ROWS * GATE_ROWS, GATE_ROWS)
    start = pl.multiple_of(group * width, width)
    copy = pltpu.make_async_copy(
        table_ref.at[pl.ds(first, GATE_ROWS), pl.ds(start, width)], picked, sem
    )
    copy.start()
    usable = lax.broadcasted_iota(jnp.int32, (1, text_k_ref.shape[0]), 1) < caption_ref[0, sample]
    for head in range(width // HD):
        cols = slice(head * HD, (head + 1) * HD)
        for block in range(SPAN * rows // BLOCK_ROWS):
            span = slice(block * BLOCK_ROWS, (block + 1) * BLOCK_ROWS)
            query = block_of(moved_ref, block, 0, rows, cols)
            own = dot_keys(query, whole(moved_ref, 1, rows, cols))
            text = jnp.where(usable, dot_keys(query, text_k_ref[:, cols]), -1e30)
            row_max = jnp.maximum(
                jnp.max(own, axis=1, keepdims=True), jnp.max(text, axis=1, keepdims=True)
            )
            own = jnp.exp2((own - row_max) * SCALE)
            text = jnp.exp2((text - row_max) * SCALE)
            max_ref[head, span, :] = row_max
            total_ref[head, span, :] = jnp.sum(own, axis=1, keepdims=True) + jnp.sum(
                text, axis=1, keepdims=True
            )
            acc_ref[span, cols] = dot_values(own, whole(moved_ref, 2, rows, cols)) + dot_values(
                text, text_v_ref[:, cols]
            )
    copy.wait()
    row = lax.broadcasted_iota(jnp.int32, (GATE_ROWS, 1), 0) == level - first
    gate_ref[...] = jnp.sum(
        jnp.where(row, picked[...].astype(jnp.float32), 0.0), axis=0, keepdims=True
    )


def attend_own(caption_len, noise_level, moved, text_k, text_v, table):
    rows = moved.shape[1] // 3 * SPAN
    width = moved.shape[2]
    stat = jax.ShapeDtypeStruct((width // HD, rows, 1), jnp.float32)
    return pl.pallas_call(
        own_kernel,
        out_shape=(
            jax.ShapeDtypeStruct((rows, width), jnp.float32),
            stat,
            stat,
            jax.ShapeDtypeStruct((1, width), jnp.float32),
        ),
        in_specs=[SMEM, SMEM, VMEM, VMEM, VMEM, HBM],
        out_specs=(VMEM,) * 4,
        scratch_shapes=[
            pltpu.VMEM((GATE_ROWS, width), table.dtype),
            pltpu.SemaphoreType.DMA,
        ],
        compiler_params=PARAMS,
        cost_estimate=pl.CostEstimate(
            flops=336_000_000, bytes_accessed=1_500_000, transcendentals=655_360
        ),
    )(
        caption_len, noise_level, moved, text_k, text_v,
        pltpu.with_memory_space_constraint(table, pltpu.HBM),
    )


def prior_kernel(moved_ref, prior_ref, acc_ref, max_ref, total_ref, gate_ref, out_ref):
    rows = prior_ref.shape[1] // 2
    width = moved_ref.shape[2]
    has_prior = lax.axis_index("stretch") > 0
    for head in range(width // HD):
        cols = slice(head * HD, (head + 1) * HD)
        gate = gate_ref[:, cols]
        for block in range(SPAN * rows // BLOCK_ROWS):
            span = slice(block * BLOCK_ROWS, (block + 1) * BLOCK_ROWS)
            query = block_of(moved_ref, block, 0, rows, cols)
            prior = dot_keys(query, whole(prior_ref, 0, rows, cols))
            own_max = max_ref[head, span, :]
            row_max = jnp.maximum(own_max, jnp.max(prior, axis=1, keepdims=True))
            row_max = jnp.where(has_prior, row_max, own_max)
            shift = jnp.exp2((own_max - row_max) * SCALE)
            prior = jnp.exp2((prior - jnp.where(has_prior, row_max, 1e30)) * SCALE)
            total = total_ref[head, span, :] * shift + jnp.sum(prior, axis=1, keepdims=True)
            result = acc_ref[span, cols] * shift + dot_values(
                prior, whole(prior_ref, 1, rows, cols)
            )
            attended = (result / total).astype(jnp.bfloat16).astype(jnp.float32)
            gated = (gate * attended).astype(out_ref.dtype)
            count = BLOCK_ROWS // rows
            out_ref[block * count : (block + 1) * count, :, cols] = gated.reshape(count, rows, HD)


def attend_prior(moved, prior, *own):
    rows = prior.shape[1] // 2
    return pl.pallas_call(
        prior_kernel,
        out_shape=jax.ShapeDtypeStruct((SPAN, rows, moved.shape[2]), jnp.bfloat16),
        in_specs=[VMEM] * (2 + len(own)),
        out_specs=VMEM,
        compiler_params=PARAMS,
        cost_estimate=pl.CostEstimate(
            flops=268_000_000, bytes_accessed=2_000_000, transcendentals=524_288
        ),
    )(moved, prior, *own)


def swap(blocks):
    videos = lax.axis_size("seq") // SPAN
    groups = [[video * SPAN + i for i in range(SPAN)] for video in range(videos)]
    return lax.all_to_all(blocks, "seq", 0, 0, axis_index_groups=groups)


def body(query, keys, values, text_keys, text_values, caption_len, noise_level, gate_table):
    tok_rows = query.shape[1]
    moved = swap(split(query[0], keys[0], values[0]))
    last = lax.axis_size("stretch") - 1
    prior = lax.ppermute(moved[:, tok_rows:], "stretch", [(i, i + 1) for i in range(last)])
    own = attend_own(
        caption_len, noise_level, moved, text_keys[0, 0], text_values[0, 0], gate_table
    )
    mixed = attend_prior(moved, prior, *own)
    return merge(swap(mixed))[None]


def solution(mesh):
    placed = (
        P("stretch", "seq", None),
        P("stretch", "seq", None),
        P("stretch", "seq", None),
        P("stretch", "seq", None, None),
        P("stretch", "seq", None, None),
        P("stretch", None),
        P("stretch", None),
        P(),
    )
    return jax.shard_map(
        body, mesh=mesh, in_specs=placed, out_specs=P("stretch", "seq", None), check_vma=False
    )
```

time: 61.8 us -> 59.2 us (0.958)
  local copies, waits for them, and re-layouts: 5.48 us -> 0.68 us
  Pallas kernels: 3.22 us -> 6.85 us
  between operations: 2.07 us -> 0.07 us
  waiting for transfers between devices: 3.78 us -> 5.11 us
  other arithmetic: 0.79 us -> 0 us
    pallas_call x1 -> x4, Pallas kernels: 3.22 us -> 6.85 us  [the longest x1 2.78 us: attend_own(): pl.pallas_call(own_kernel, out_shape=(jax.ShapeDtypeStruct((rows, width),...]
    unnamed x15 -> x8, local copies, waits for them, and re-layouts: 2.7 us -> 0.65 us
    dynamic_slice x2 -> x0, local copies, waits for them, and re-layouts: 1.4 us -> none  [the longest x1 0.77 us: body(): lax.dynamic_slice(gate_table, (level, group * group_width), (1, group_wid...]
    ppermute x1, waiting for transfers between devices: 3.78 us -> 5.11 us  [body(): lax.ppermute(moved[:, tok_rows:], 'stretch', [(i, i + 1) for i in range(l...]
    reshape x1 -> x0, local copies, waits for them, and re-layouts: 0.83 us -> none  [body(): return returned.transpose(1, 0, 2).reshape(1, tok_rows, width)]
    another operation x2 -> x0, other arithmetic: 0.79 us -> none  [the longest x1 0.71 us: body(): info = jnp.stack([caption, stretch_index]).astype(jnp.int32)]
  transfers between devices with their start and end apart: 1 -> 1, of which waited for: 1 -> 1; matrix products, arithmetic and copies ran while one was open for 4% -> 0% of each run, Pallas kernels for 0% -> 5%
where the time goes in v2:
time: 59.2 us; the launch traced here: 58.9 us
  blocking collectives  44.1 us (74%)
  Pallas kernels  6.85 us (12%)
  waiting for transfers between devices  5.11 us (9%)
  starting transfers between devices  2.05 us (3%)
  local copies, waits for them, and re-layouts  0.68 us (1%)
    all_to_all x2, blocking collectives, swap(): return lax.all_to_all(blocks, 'seq', 0, 0, axis_index_groups=groups)  44.1 us
    ppermute x1, waiting for transfers between devices, body(): lax.ppermute(moved[:, tok_rows:], 'stretch', [(i, i + 1) for i in range(l...  5.11 us
    pallas_call x1, Pallas kernels, attend_own(): pl.pallas_call(own_kernel, out_shape=(jax.ShapeDtypeStruct((rows, width),...  2.78 us
    ppermute x1, starting transfers between devices, body(): lax.ppermute(moved[:, tok_rows:], 'stretch', [(i, i + 1) for i in range(l...  2.05 us
    pallas_call x1, Pallas kernels, attend_prior(): pl.pallas_call(prior_kernel, out_shape=jax.ShapeDtypeStruct((SPAN, rows,...  1.73 us
    pallas_call x1, Pallas kernels, split(): pl.pallas_call(split_kernel, out_shape=jax.ShapeDtypeStruct((SPAN, 3 * ro...  1.52 us
  transfers between devices with their start and end apart: 1, of which 1 were waited for; matrix products, arithmetic and copies ran while one was open for 0% of the time, Pallas kernels for 5%

profile of v2, /device:TPU:72, one launch (start us, length us, event | category | flops | bytes accessed | tf_op | source)
XLA Modules:
  0.0 58.9 jit_solution(7667260196849616054)
XLA Ops:
  0.0 1.5 %shard_map.82 = bf16[16,96,256]{2,1,0:T(8,128)(2,1)S(1)} custom-call(bf16[32,4096]{1,0:T(8,128)(2,1)} %bitcast.8, bf16[32,4096]{1,0:T(8,128)(2,1)} %bitcast.9, bf16[32,4096]{1,0:T(8,128)(2,1)} %bitcast.10), custom_call_target="tpu_custom_call" | custom-call | tf_op jit(solution)/shard_map/pallas_call | solution.py:41
  1.5 29.8 %all_to_all.10.moved_ref = bf16[16,96,256]{2,1,0:T(8,128)(2,1)S(1)} all-to-all(bf16[16,96,256]{2,1,0:T(8,128)(2,1)S(1)} %shard_map.82), channel_id=1, replica_groups={{0,1,2,3,4,5,6,7,8,9,10,11,12,13,14,15},{16,17,18,19,20,21,22,23,24,25,..., dimensions={0} | all-to-all | bytes 1572864 | tf_op jit(solution)/shard_map/all_to_all | solution.py:208
  31.4 0.0 copy-start
  31.4 0.0 copy-start.1
  31.4 2.1 %collective-permute-start = (bf16[16,64,256]{2,1,0:T(8,128)(2,1)S(1)}, bf16[16,64,256]{2,1,0:T(8,128)(2,1)S(1)}, u32[]{:S(2)}, u32[]{:S(2)}) collective-permute-start(bf16[16,64,256]{2,1,0:T(8,128)(2,1)S(1)} %slice.4), channel_id=1, source_target_pairs={{0,64},{64,128},{128,192},{192,256},{256,320},{320,384},{384,448},... | collective-permute-start | bytes 1572872 | tf_op jit(solution)/shard_map/ppermute | solution.py:215
  33.5 0.0 copy-start.2
  33.5 0.0 copy-start.3
  33.5 0.0 copy-done
  33.5 0.0 copy-done.1
  33.5 0.6 %copy-done.2 = s32[1,4]{1,0:T(1,128)S(1)} copy-done((s32[1,4]{1,0:T(1,128)S(1)}, s32[1,4]{1,0:T(1,128)}, u32[]{:S(2)}) %copy-start.2) | copy-done | bytes 40
  34.1 0.0 copy-done.3
  34.1 2.8 %shard_map.83 = (f32[512,256]{1,0:T(8,128)S(1)}, f32[2,512,1]{2,1,0:T(8,128)S(1)}, f32[2,512,1]{2,1,0:T(8,128)S(1)}, f32[1,256]{1,0:T(1,128)S(1)}) custom-call(s32[1,4]{1,0:T(1,128)S(1)} %copy-done.2, s32[1,4]{1,0:T(1,128)S(1)} %copy-done.3, bf16[16,96,256]{2,1,0:T(8,128)(2,1)S(1)} %all_to_all.10.moved_ref, bf16[128,256]{1,0:T(8,128)(2,1)S(1)} %bitcast.6, ...), custom_call_target="tpu_custom_call" | custom-call | flops 336000000 | bytes 1500000 | tf_op jit(solution)/shard_map/pallas_call | solution.py:141
  36.9 5.1 %collective-permute-done.prior_ref = bf16[16,64,256]{2,1,0:T(8,128)(2,1)S(1)} collective-permute-done((bf16[16,64,256]{2,1,0:T(8,128)(2,1)S(1)}, bf16[16,64,256]{2,1,0:T(8,128)(2,1)S(1)}, u32[]{:S(2)}, u32[]{:S(2)}) %collective-permute-start) | collective-permute-done | bytes 524320 | tf_op jit(solution)/shard_map/ppermute | solution.py:215
  42.0 1.7 %shard_map.84 = bf16[16,32,256]{2,1,0:T(8,128)(2,1)S(1)} custom-call(bf16[16,96,256]{2,1,0:T(8,128)(2,1)S(1)} %all_to_all.10.moved_ref, bf16[16,64,256]{2,1,0:T(8,128)(2,1)S(1)} %collective-permute-done.prior_ref, f32[512,256]{1,0:T(8,128)S(1)} %get-tuple-element.9.acc_ref, f32[2,512,1]{2,1,0:T(8,128)S(1)} %get-tuple-element.10.max_ref, ...), custom_call_target="tpu_custom_call" | custom-call | flops 268000000 | bytes 2000000 | tf_op jit(solution)/shard_map/pallas_call | solution.py:193
  43.8 14.3 %all_to_all.11.blocks_ref = bf16[16,32,256]{2,1,0:T(8,128)(2,1)S(1)} all-to-all(bf16[16,32,256]{2,1,0:T(8,128)(2,1)S(1)} %shard_map.84), channel_id=1, replica_groups={{0,1,2,3,4,5,6,7,8,9,10,11,12,13,14,15},{16,17,18,19,20,21,22,23,24,25,..., dimensions={0} | all-to-all | bytes 524288 | tf_op jit(solution)/shard_map/all_to_all | solution.py:208
  58.1 0.8 %shard_map.85 = bf16[32,4096]{1,0:T(8,128)(2,1)} custom-call(bf16[16,32,256]{2,1,0:T(8,128)(2,1)S(1)} %all_to_all.11.blocks_ref), custom_call_target="tpu_custom_call" | custom-call | tf_op jit(solution)/shard_map/pallas_call | solution.py:66
  (1 shorter events, 0.0 us)
Async XLA Ops:
  31.4 2.1 %copy-start = (bf16[1,1,128,256]{3,2,1,0:T(8,128)(2,1)S(1)}, bf16[1,1,128,256]{3,2,1,0:T(8,128)(2,1)}, u32[]{:S(2)}) copy-start(bf16[1,1,128,256]{3,2,1,0:T(8,128)(2,1)} %param.11) | copy-start | bytes 196612
  31.4 2.1 %copy-start.1 = (bf16[1,1,128,256]{3,2,1,0:T(8,128)(2,1)S(1)}, bf16[1,1,128,256]{3,2,1,0:T(8,128)(2,1)}, u32[]{:S(2)}) copy-start(bf16[1,1,128,256]{3,2,1,0:T(8,128)(2,1)} %param.12) | copy-start | bytes 196612
  31.4 10.6 %collective-permute-start = (bf16[16,64,256]{2,1,0:T(8,128)(2,1)S(1)}, bf16[16,64,256]{2,1,0:T(8,128)(2,1)S(1)}, u32[]{:S(2)}, u32[]{:S(2)}) collective-permute-start(bf16[16,64,256]{2,1,0:T(8,128)(2,1)S(1)} %slice.4), channel_id=1, source_target_pairs={{0,64},{64,128},{128,192},{192,256},{256,320},{320,384},{384,448},... | collective-permute-start | bytes 1572872 | tf_op jit(solution)/shard_map/ppermute | solution.py:215
  33.5 0.7 %copy-start.2 = (s32[1,4]{1,0:T(1,128)S(1)}, s32[1,4]{1,0:T(1,128)}, u32[]{:S(2)}) copy-start(s32[1,4]{1,0:T(1,128)} %caption_ref.1) | copy-start | bytes 52
  33.5 0.7 %copy-start.3 = (s32[1,4]{1,0:T(1,128)S(1)}, s32[1,4]{1,0:T(1,128)}, u32[]{:S(2)}) copy-start(s32[1,4]{1,0:T(1,128)} %level_ref.1) | copy-start | bytes 52

commit v3 on v2

v3 whole, which is shorter than its diff:
```python
import math

import jax
import jax.numpy as jnp
from jax import lax
from jax.experimental import pallas as pl
from jax.experimental.pallas import tpu as pltpu
from jax.sharding import PartitionSpec as P

HD = 128
SPAN = 16
GATE_ROWS = 16
TILE_ROWS = 8
BLOCK_ROWS = 256
SCALE = math.log2(math.e) / math.sqrt(HD)
NT = (((1,), (1,)), ((), ()))
VMEM = pl.BlockSpec(memory_space=pltpu.VMEM)
SMEM = pl.BlockSpec(memory_space=pltpu.SMEM)
HBM = pl.BlockSpec(memory_space=pltpu.HBM)
PARAMS = pltpu.CompilerParams(vmem_limit_bytes=32 * 1024 * 1024)


def tiles_of(array):
    rows, width = array.shape
    view = array.reshape(rows // TILE_ROWS, TILE_ROWS, SPAN, width // SPAN // HD, HD)
    return view.transpose(0, 2, 3, 1, 4)


def rows_of(tiles):
    lead = tiles.shape[:-4]
    strips, across, tile_rows, tile_cols = tiles.shape[-4:]
    view = jnp.swapaxes(tiles, -3, -2)
    return view.reshape(*lead, strips * tile_rows, across * tile_cols)


def split_kernel(query_ref, keys_ref, values_ref, out_ref, sems):
    copies = []
    for part, ref in enumerate((query_ref, keys_ref, values_ref)):
        for strip in range(ref.shape[0]):
            copy = pltpu.make_async_copy(
                ref.at[strip], out_ref.at[:, part, strip], sems.at[part, strip]
            )
            copy.start()
            copies.append(copy)
    for copy in copies:
        copy.wait()


def split(*arrays):
    tiles = [pltpu.with_memory_space_constraint(tiles_of(array), pltpu.HBM) for array in arrays]
    strips, groups, *tile = tiles[0].shape
    return pl.pallas_call(
        split_kernel,
        out_shape=jax.ShapeDtypeStruct((groups, len(tiles), strips, *tile), tiles[0].dtype),
        in_specs=[HBM] * len(tiles),
        out_specs=VMEM,
        scratch_shapes=[pltpu.SemaphoreType.DMA((len(tiles), strips))],
        compiler_params=PARAMS,
    )(*tiles)


def merge_kernel(blocks_ref, out_ref, sems):
    copies = []
    for strip in range(out_ref.shape[0]):
        copy = pltpu.make_async_copy(blocks_ref.at[:, strip], out_ref.at[strip], sems.at[strip])
        copy.start()
        copies.append(copy)
    for copy in copies:
        copy.wait()


def merge(blocks):
    groups, rows, width = blocks.shape
    view = blocks.reshape(groups, rows // TILE_ROWS, TILE_ROWS, width // HD, HD)
    view = view.transpose(0, 1, 3, 2, 4)
    strips = view.shape[1]
    out = pl.pallas_call(
        merge_kernel,
        out_shape=jax.ShapeDtypeStruct((strips, groups, *view.shape[2:]), blocks.dtype),
        in_specs=[VMEM],
        out_specs=HBM,
        scratch_shapes=[pltpu.SemaphoreType.DMA((strips,))],
        compiler_params=PARAMS,
    )(view)
    return out.transpose(0, 3, 1, 2, 4).reshape(rows, groups * width)


def pick_kernel(caption_ref, level_ref, table_ref, gate_ref, bias_ref, picked, sem):
    width = gate_ref.shape[1]
    seq_index = lax.axis_index("seq")
    sample = seq_index // SPAN
    level = level_ref[0, sample]
    first = pl.multiple_of(level // GATE_ROWS * GATE_ROWS, GATE_ROWS)
    start = pl.multiple_of(seq_index % SPAN * width, width)
    copy = pltpu.make_async_copy(
        table_ref.at[pl.ds(first, GATE_ROWS), pl.ds(start, width)], picked, sem
    )
    copy.start()
    slot = lax.broadcasted_iota(jnp.int32, bias_ref.shape, 1)
    bias_ref[...] = jnp.where(slot < caption_ref[0, sample], 0.0, -1e30)
    copy.wait()
    row = lax.broadcasted_iota(jnp.int32, (GATE_ROWS, 1), 0) == level - first
    gate_ref[...] = jnp.sum(
        jnp.where(row, picked[...].astype(jnp.float32), 0.0), axis=0, keepdims=True
    )


def pick(caption_len, noise_level, table, slots):
    width = table.shape[1] // SPAN
    return pl.pallas_call(
        pick_kernel,
        out_shape=(
            jax.ShapeDtypeStruct((1, width), jnp.float32),
            jax.ShapeDtypeStruct((1, slots), jnp.float32),
        ),
        in_specs=[SMEM, SMEM, HBM],
        out_specs=(VMEM, VMEM),
        scratch_shapes=[pltpu.VMEM((GATE_ROWS, width), table.dtype), pltpu.SemaphoreType.DMA],
        compiler_params=PARAMS,
    )(caption_len, noise_level, pltpu.with_memory_space_constraint(table, pltpu.HBM))


def is_odd():
    return lax.axis_index("stretch") % 2 == 1


def block_of(ref, block, part, rows, cols):
    count = BLOCK_ROWS // rows
    tile = ref[block * count : (block + 1) * count, part * rows : (part + 1) * rows, cols]
    return tile.reshape(BLOCK_ROWS, HD)


def whole(ref, part, rows, cols):
    return ref[:, part * rows : (part + 1) * rows, cols].reshape(ref.shape[0] * rows, HD)


def dot_keys(query, keys):
    return lax.dot_general(query, keys, NT, preferred_element_type=jnp.float32)


def dot_values(weights, values):
    return jnp.dot(weights.astype(jnp.bfloat16), values, preferred_element_type=jnp.float32)


def row_top(scores):
    return jnp.max(scores, axis=1, keepdims=True)


def row_sum(weights):
    return jnp.sum(weights, axis=1, keepdims=True)


def blocks_in(moved_ref):
    rows = moved_ref.shape[1] // 3
    for head in range(moved_ref.shape[2] // HD):
        for block in range(SPAN * rows // BLOCK_ROWS):
            span = slice(block * BLOCK_ROWS, (block + 1) * BLOCK_ROWS)
            yield head, slice(head * HD, (head + 1) * HD), block, span, rows


def store(out_ref, block, rows, cols, result, total, gate_ref):
    attended = (result / total).astype(jnp.bfloat16).astype(jnp.float32)
    gated = (gate_ref[:, cols] * attended).astype(out_ref.dtype)
    count = BLOCK_ROWS // rows
    out_ref[block * count : (block + 1) * count, :, cols] = gated.reshape(count, rows, HD)


def own_kernel(moved_ref, text_k_ref, text_v_ref, bias_ref, acc_ref, max_ref, total_ref):
    if True:
        for head, cols, block, span, rows in blocks_in(moved_ref):
            query = block_of(moved_ref, block, 0, rows, cols)
            own = dot_keys(query, whole(moved_ref, 1, rows, cols))
            text = dot_keys(query, text_k_ref[:, cols]) + bias_ref[...]
            top = jnp.maximum(row_top(own), row_top(text))
            own = jnp.exp2((own - top) * SCALE)
            text = jnp.exp2((text - top) * SCALE)
            max_ref[head, span, :] = top
            total_ref[head, span, :] = row_sum(own) + row_sum(text)
            acc_ref[span, cols] = dot_values(own, whole(moved_ref, 2, rows, cols)) + dot_values(
                text, text_v_ref[:, cols]
            )


def attend_own(moved, text_k, text_v, bias):
    rows = moved.shape[1] // 3 * SPAN
    width = moved.shape[2]
    stat = jax.ShapeDtypeStruct((width // HD, rows, 1), jnp.float32)
    return pl.pallas_call(
        own_kernel,
        out_shape=(jax.ShapeDtypeStruct((rows, width), jnp.float32), stat, stat),
        in_specs=[VMEM] * 4,
        out_specs=(VMEM,) * 3,
        compiler_params=PARAMS,
        cost_estimate=pl.CostEstimate(
            flops=336_000_000, bytes_accessed=1_500_000, transcendentals=655_360
        ),
    )(moved, text_k, text_v, bias)


def last_kernel(
    moved_ref, near_ref, far_ref, text_k_ref, text_v_ref, bias_ref, gate_ref,
    acc_ref, max_ref, total_ref, out_ref,
):
    @pl.when(is_odd())
    def _():
        add_prior(
            moved_ref, near_ref, True, acc_ref, max_ref, total_ref, gate_ref, out_ref
        )

    @pl.when(jnp.logical_not(is_odd()))
    def _():
        has_prior = lax.axis_index("stretch") > 0
        add_prior(
            moved_ref, far_ref, has_prior, acc_ref, max_ref, total_ref, gate_ref, out_ref
        )


def attend_all(
    moved_ref, prior_ref, has_prior, text_k_ref, text_v_ref, bias_ref, gate_ref, out_ref
):
    for head, cols, block, span, rows in blocks_in(moved_ref):
        query = block_of(moved_ref, block, 0, rows, cols)
        own = dot_keys(query, whole(moved_ref, 1, rows, cols))
        prior = dot_keys(query, whole(prior_ref, 0, rows, cols))
        text = dot_keys(query, text_k_ref[:, cols]) + bias_ref[...]
        top = jnp.maximum(row_top(own), row_top(text))
        top = jnp.where(has_prior, jnp.maximum(top, row_top(prior)), top)
        own = jnp.exp2((own - top) * SCALE)
        text = jnp.exp2((text - top) * SCALE)
        prior = jnp.exp2((prior - jnp.where(has_prior, top, 1e30)) * SCALE)
        total = row_sum(own) + row_sum(text) + row_sum(prior)
        result = (
            dot_values(own, whole(moved_ref, 2, rows, cols))
            + dot_values(text, text_v_ref[:, cols])
            + dot_values(prior, whole(prior_ref, 1, rows, cols))
        )
        store(out_ref, block, rows, cols, result, total, gate_ref)


def add_prior(moved_ref, prior_ref, has_prior, acc_ref, max_ref, total_ref, gate_ref, out_ref):
    for head, cols, block, span, rows in blocks_in(moved_ref):
        query = block_of(moved_ref, block, 0, rows, cols)
        prior = dot_keys(query, whole(prior_ref, 0, rows, cols))
        own_top = max_ref[head, span, :]
        top = jnp.where(has_prior, jnp.maximum(own_top, row_top(prior)), own_top)
        shift = jnp.exp2((own_top - top) * SCALE)
        prior = jnp.exp2((prior - jnp.where(has_prior, top, 1e30)) * SCALE)
        total = total_ref[head, span, :] * shift + row_sum(prior)
        result = acc_ref[span, cols] * shift + dot_values(
            prior, whole(prior_ref, 1, rows, cols)
        )
        store(out_ref, block, rows, cols, result, total, gate_ref)


def attend_last(moved, *rest):
    return pl.pallas_call(
        last_kernel,
        out_shape=jax.ShapeDtypeStruct(
            (SPAN, moved.shape[1] // 3, moved.shape[2]), jnp.bfloat16
        ),
        in_specs=[VMEM] * (1 + len(rest)),
        out_specs=VMEM,
        compiler_params=PARAMS,
        cost_estimate=pl.CostEstimate(
            flops=604_000_000, bytes_accessed=3_000_000, transcendentals=1_179_648
        ),
    )(moved, *rest)


def swap(blocks):
    videos = lax.axis_size("seq") // SPAN
    groups = [[video * SPAN + i for i in range(SPAN)] for video in range(videos)]
    return lax.all_to_all(blocks, "seq", 0, 0, axis_index_groups=groups)


def body(query, keys, values, text_keys, text_values, caption_len, noise_level, gate_table):
    tok_rows = query.shape[1]
    stretches = lax.axis_size("stretch")

    def exchanged():
        return swap(split(query[0], keys[0], values[0]))

    def shifted(blocks, first):
        route = [(i, i + 1) for i in range(first, stretches - 1, 2)]
        return lax.ppermute(blocks[:, tok_rows:], "stretch", route)

    def rows_view(tiles):
        return rows_of(tiles).reshape(SPAN, 3 * tok_rows, -1)

    odd = is_odd()
    shape = jax.eval_shape(exchanged)
    early = lax.cond(odd, exchanged, lambda: jnp.zeros(shape.shape, shape.dtype))
    far = shifted(rows_view(early), 1)
    early, caption_len, noise_level = lax.optimization_barrier((early, caption_len, noise_level))
    gate, bias = pick(caption_len, noise_level, gate_table, text_keys.shape[2])
    odd, gate, bias = lax.optimization_barrier((odd, gate, bias))
    moved = rows_view(lax.cond(odd, lambda x: x, lambda x: exchanged(), early))
    near = shifted(moved, 0)
    text = (text_keys[0, 0], text_values[0, 0], bias)
    own = attend_own(moved, *text)
    mixed = attend_last(moved, near, far, *text, gate, *own)
    return merge(swap(mixed))[None]


def solution(mesh):
    placed = (
        P("stretch", "seq", None),
        P("stretch", "seq", None),
        P("stretch", "seq", None),
        P("stretch", "seq", None, None),
        P("stretch", "seq", None, None),
        P("stretch", None),
        P("stretch", None),
        P(),
    )
    return jax.shard_map(
        body, mesh=mesh, in_specs=placed, out_specs=P("stretch", "seq", None), check_vma=False
    )
```

time: 59.2 us -> 53.5 us (0.904)
  the two profiles are of different devices: /device:TPU:72 before, /device:TPU:1 now
where the time goes in v3:
time: 53.5 us; the launch traced here: 53.2 us
  blocking collectives  41.2 us (77%)
  Pallas kernels  6.76 us (13%)
  starting transfers between devices  2.61 us (5%)
  waiting for transfers between devices  2.37 us (4%)
    all_to_all x2, blocking collectives, swap(): return lax.all_to_all(blocks, 'seq', 0, 0, axis_index_groups=groups)  41.2 us
    ppermute x2, starting transfers between devices, shifted(): return lax.ppermute(blocks[:, tok_rows:], 'stretch', route)  2.61 us
    ppermute x2, waiting for transfers between devices, shifted(): return lax.ppermute(blocks[:, tok_rows:], 'stretch', route)  2.37 us
    pallas_call x1, Pallas kernels, attend_own(): pl.pallas_call(own_kernel, out_shape=(jax.ShapeDtypeStruct((rows, width),...  1.76 us
    pallas_call x1, Pallas kernels, attend_last(): pl.pallas_call(last_kernel, out_shape=jax.ShapeDtypeStruct((SPAN, moved.s...  1.72 us
    pallas_call x1, Pallas kernels, pick(): pl.pallas_call(pick_kernel, out_shape=(jax.ShapeDtypeStruct((1, width), j...  1.29 us
    pallas_call x1, Pallas kernels, split(): pl.pallas_call(split_kernel, out_shape=jax.ShapeDtypeStruct((groups, len(...  1.26 us
  transfers between devices with their start and end apart: 2, of which 2 were waited for; matrix products, arithmetic and copies ran while one was open for 0% of the time, Pallas kernels for 6%

profile of v3, /device:TPU:1, one launch (start us, length us, event | category | flops | bytes accessed | tf_op | source)
XLA Modules:
  0.0 53.2 jit_solution(2993350396692085664)
XLA Ops:
  0.0 26.8 %conditional.2 = (bf16[16,3,4,2,8,128]{5,4,3,2,1,0:T(8,128)(2,1)S(1)}) conditional(s32[]{:T(128)} %convert_element_type.6, () %tuple.19, (bf16[1,32,4096]{2,1,0:T(8,128)(2,1)}, bf16[1,32,4096]{2,1,0:T(8,128)(2,1)}, bf16[1,32,4096]{2,1,0:T(8,128)(2,1)}) %tuple.20), branch_computations={%region_0.1_spmd, %region_1.2_spmd} | conditional | bytes 1572872 | solution.py:292
  0.0 1.3 %branch_1_fun.1 = bf16[16,3,4,2,8,128]{5,4,3,2,1,0:T(8,128)(2,1)S(1)} custom-call(bf16[4,16,2,8,128]{4,3,2,1,0:T(8,128)(2,1)} %bitcast.41, bf16[4,16,2,8,128]{4,3,2,1,0:T(8,128)(2,1)} %bitcast.43, bf16[4,16,2,8,128]{4,3,2,1,0:T(8,128)(2,1)} %bitcast.45), custom_call_target="tpu_custom_call" | custom-call | tf_op jit(solution)/shard_map/cond/branch_1_fun/pallas_call | solution.py:52
  1.3 25.5 %all_to_all.13 = bf16[16,3,4,2,8,128]{5,4,3,2,1,0:T(8,128)(2,1)S(1)} all-to-all(bf16[16,3,4,2,8,128]{5,4,3,2,1,0:T(8,128)(2,1)S(1)} %branch_1_fun.1), channel_id=1, replica_groups={{0,1,2,3,4,5,6,7,8,9,10,11,12,13,14,15},{16,17,18,19,20,21,22,23,24,25,..., dimensions={0} | all-to-all | bytes 1572864 | tf_op jit(solution)/shard_map/cond/branch_1_fun/all_to_all | solution.py:273
  26.8 0.0 copy-start.2
  26.8 0.0 copy-start.3
  26.8 1.3 %collective-permute-start.1 = (bf16[16,64,256]{2,1,0:T(8,128)(2,1)S(1)}, bf16[16,64,256]{2,1,0:T(8,128)(2,1)S(1)}, u32[]{:S(2)}, u32[]{:S(2)}) collective-permute-start(bf16[16,64,256]{2,1,0:T(8,128)(2,1)S(1)} %slice.9), channel_id=1, source_target_pairs={{64,128},{192,256},{320,384},{65,129},{193,257},{321,385},{66,130}... | collective-permute-start | bytes 1572872 | tf_op jit(solution)/shard_map/ppermute | solution.py:285
  28.1 0.0 copy-done.2
  28.1 0.0 copy-done.3
  28.2 1.3 %shard_map.82 = (f32[1,256]{1,0:T(1,128)S(1)}, f32[1,128]{1,0:T(1,128)S(1)}) custom-call(s32[1,4]{1,0:T(1,128)S(1)} %copy-done.2, s32[1,4]{1,0:T(1,128)S(1)} %copy-done.3, bf16[32,4096]{1,0:T(8,128)(2,1)} %table_ref.1), custom_call_target="tpu_custom_call" | custom-call | tf_op jit(solution)/shard_map/pallas_call | solution.py:110
  29.5 0.0 copy-start
  29.5 0.0 copy-start.1
  29.5 1.3 %collective-permute-start = (bf16[16,64,256]{2,1,0:T(8,128)(2,1)S(1)}, bf16[16,64,256]{2,1,0:T(8,128)(2,1)S(1)}, u32[]{:S(2)}, u32[]{:S(2)}) collective-permute-start(bf16[16,64,256]{2,1,0:T(8,128)(2,1)S(1)} %slice.8), channel_id=1, source_target_pairs={{0,64},{128,192},{256,320},{384,448},{1,65},{129,193},{257,321},{3... | collective-permute-start | bytes 1572872 | tf_op jit(solution)/shard_map/ppermute | solution.py:285
  30.8 0.0 copy-done
  30.9 0.0 copy-done.1
  30.9 1.8 %shard_map.83 = (f32[512,256]{1,0:T(8,128)S(1)}, f32[2,512,1]{2,1,0:T(8,128)S(1)}, f32[2,512,1]{2,1,0:T(8,128)S(1)}) custom-call(bf16[16,96,256]{2,1,0:T(8,128)(2,1)S(1)} %bitcast.39, bf16[128,256]{1,0:T(8,128)(2,1)S(1)} %bitcast.33, bf16[128,256]{1,0:T(8,128)(2,1)S(1)} %bitcast.35, f32[1,128]{1,0:T(1,128)S(1)} %get-tuple-element.47.bias_ref), custom_call_target="tpu_custom_call" | custom-call | flops 336000000 | bytes 1500000 | tf_op jit(solution)/shard_map/pallas_call | solution.py:188
  32.6 1.6 %collective-permute-done.1.far_ref = bf16[16,64,256]{2,1,0:T(8,128)(2,1)S(1)} collective-permute-done((bf16[16,64,256]{2,1,0:T(8,128)(2,1)S(1)}, bf16[16,64,256]{2,1,0:T(8,128)(2,1)S(1)}, u32[]{:S(2)}, u32[]{:S(2)}) %collective-permute-start.1) | collective-permute-done | bytes 524320 | tf_op jit(solution)/shard_map/ppermute | solution.py:285
  34.2 0.8 %collective-permute-done.near_ref = bf16[16,64,256]{2,1,0:T(8,128)(2,1)S(1)} collective-permute-done((bf16[16,64,256]{2,1,0:T(8,128)(2,1)S(1)}, bf16[16,64,256]{2,1,0:T(8,128)(2,1)S(1)}, u32[]{:S(2)}, u32[]{:S(2)}) %collective-permute-start) | collective-permute-done | bytes 524320 | tf_op jit(solution)/shard_map/ppermute | solution.py:285
  35.0 1.7 %shard_map.84 = bf16[16,32,256]{2,1,0:T(8,128)(2,1)S(1)} custom-call(bf16[16,96,256]{2,1,0:T(8,128)(2,1)S(1)} %bitcast.40, bf16[16,64,256]{2,1,0:T(8,128)(2,1)S(1)} %collective-permute-done.near_ref, bf16[16,64,256]{2,1,0:T(8,128)(2,1)S(1)} %collective-permute-done.1.far_ref, bf16[128,256]{1,0:T(8,128)(2,1)S(1)} %bitcast.34, bf16[128,256]{1,0:T(8,128)(2,1)S(1)} %bitcast.36, ...), custom_call_target="tpu_custom_call" | custom-call | flops 604000000 | bytes 3000000 | tf_op jit(solution)/shard_map/pallas_call | solution.py:256
  36.7 15.7 %all_to_all.15 = bf16[16,32,256]{2,1,0:T(8,128)(2,1)S(1)} all-to-all(bf16[16,32,256]{2,1,0:T(8,128)(2,1)S(1)} %shard_map.84), channel_id=1, replica_groups={{0,1,2,3,4,5,6,7,8,9,10,11,12,13,14,15},{16,17,18,19,20,21,22,23,24,25,..., dimensions={0} | all-to-all | bytes 524288 | tf_op jit(solution)/shard_map/all_to_all | solution.py:273
  52.5 0.7 %shard_map.85 = bf16[4,16,2,8,128]{4,3,2,1,0:T(8,128)(2,1)} custom-call(bf16[16,4,2,8,128]{4,3,2,1,0:T(8,128)(2,1)S(1)} %bitcast.32), custom_call_target="tpu_custom_call" | custom-call | tf_op jit(solution)/shard_map/pallas_call | solution.py:77
  (3 shorter events, 0.1 us)
Async XLA Ops:
  26.8 1.4 %copy-start.2 = (s32[1,4]{1,0:T(1,128)S(1)}, s32[1,4]{1,0:T(1,128)}, u32[]{:S(2)}) copy-start(s32[1,4]{1,0:T(1,128)} %caption_ref) | copy-start | bytes 52
  26.8 1.4 %copy-start.3 = (s32[1,4]{1,0:T(1,128)S(1)}, s32[1,4]{1,0:T(1,128)}, u32[]{:S(2)}) copy-start(s32[1,4]{1,0:T(1,128)} %level_ref) | copy-start | bytes 52
  26.8 7.4 %collective-permute-start.1 = (bf16[16,64,256]{2,1,0:T(8,128)(2,1)S(1)}, bf16[16,64,256]{2,1,0:T(8,128)(2,1)S(1)}, u32[]{:S(2)}, u32[]{:S(2)}) collective-permute-start(bf16[16,64,256]{2,1,0:T(8,128)(2,1)S(1)} %slice.9), channel_id=1, source_target_pairs={{64,128},{192,256},{320,384},{65,129},{193,257},{321,385},{66,130}... | collective-permute-start | bytes 1572872 | tf_op jit(solution)/shard_map/ppermute | solution.py:285
  29.5 1.4 %copy-start = (bf16[1,1,128,256]{3,2,1,0:T(8,128)(2,1)S(1)}, bf16[1,1,128,256]{3,2,1,0:T(8,128)(2,1)}, u32[]{:S(2)}) copy-start(bf16[1,1,128,256]{3,2,1,0:T(8,128)(2,1)} %param.15) | copy-start | bytes 196612
  29.5 1.4 %copy-start.1 = (bf16[1,1,128,256]{3,2,1,0:T(8,128)(2,1)S(1)}, bf16[1,1,128,256]{3,2,1,0:T(8,128)(2,1)}, u32[]{:S(2)}) copy-start(bf16[1,1,128,256]{3,2,1,0:T(8,128)(2,1)} %param.16) | copy-start | bytes 196612
  29.5 5.5 %collective-permute-start = (bf16[16,64,256]{2,1,0:T(8,128)(2,1)S(1)}, bf16[16,64,256]{2,1,0:T(8,128)(2,1)S(1)}, u32[]{:S(2)}, u32[]{:S(2)}) collective-permute-start(bf16[16,64,256]{2,1,0:T(8,128)(2,1)S(1)} %slice.8), channel_id=1, source_target_pairs={{0,64},{128,192},{256,320},{384,448},{1,65},{129,193},{257,321},{3... | collective-permute-start | bytes 1572872 | tf_op jit(solution)/shard_map/ppermute | solution.py:285

commit v4 on v3

v4 whole, which is shorter than its diff:
```python
import math

import jax
import jax.numpy as jnp
from jax import lax
from jax.experimental import pallas as pl
from jax.experimental.pallas import tpu as pltpu
from jax.sharding import PartitionSpec as P

HD = 128
SPAN = 16
GATE_ROWS = 16
TILE_ROWS = 8
SCALE = math.log2(math.e) / math.sqrt(HD)
NT = (((1,), (1,)), ((), ()))
TN = (((0,), (0,)), ((), ()))
VMEM = pl.BlockSpec(memory_space=pltpu.VMEM)
SMEM = pl.BlockSpec(memory_space=pltpu.SMEM)
HBM = pl.BlockSpec(memory_space=pltpu.HBM)
PARAMS = pltpu.CompilerParams(vmem_limit_bytes=32 * 1024 * 1024)


def tiles_of(array):
    rows, width = array.shape
    view = array.reshape(rows // TILE_ROWS, TILE_ROWS, SPAN, width // SPAN // HD, HD)
    return view.transpose(0, 2, 3, 1, 4)


def rows_of(tiles):
    lead = tiles.shape[:-4]
    strips, across, tile_rows, tile_cols = tiles.shape[-4:]
    view = jnp.swapaxes(tiles, -3, -2)
    return view.reshape(*lead, strips * tile_rows, across * tile_cols)


def split_kernel(query_ref, keys_ref, values_ref, out_ref, sems):
    copies = []
    for part, ref in enumerate((query_ref, keys_ref, values_ref)):
        for strip in range(ref.shape[0]):
            copy = pltpu.make_async_copy(
                ref.at[strip], out_ref.at[:, part, strip], sems.at[part, strip]
            )
            copy.start()
            copies.append(copy)
    for copy in copies:
        copy.wait()


def split(*arrays):
    tiles = [pltpu.with_memory_space_constraint(tiles_of(array), pltpu.HBM) for array in arrays]
    strips, groups, *tile = tiles[0].shape
    return pl.pallas_call(
        split_kernel,
        out_shape=jax.ShapeDtypeStruct((groups, len(tiles), strips, *tile), tiles[0].dtype),
        in_specs=[HBM] * len(tiles),
        out_specs=VMEM,
        scratch_shapes=[pltpu.SemaphoreType.DMA((len(tiles), strips))],
        compiler_params=PARAMS,
    )(*tiles)


def merge_kernel(blocks_ref, out_ref, sems):
    copies = []
    for strip in range(out_ref.shape[0]):
        copy = pltpu.make_async_copy(blocks_ref.at[:, strip], out_ref.at[strip], sems.at[strip])
        copy.start()
        copies.append(copy)
    for copy in copies:
        copy.wait()


def merge(blocks):
    groups, rows, width = blocks.shape
    view = blocks.reshape(groups, rows // TILE_ROWS, TILE_ROWS, width // HD, HD)
    view = view.transpose(0, 1, 3, 2, 4)
    strips = view.shape[1]
    out = pl.pallas_call(
        merge_kernel,
        out_shape=jax.ShapeDtypeStruct((strips, groups, *view.shape[2:]), blocks.dtype),
        in_specs=[VMEM],
        out_specs=HBM,
        scratch_shapes=[pltpu.SemaphoreType.DMA((strips,))],
        compiler_params=PARAMS,
    )(view)
    return out.transpose(0, 3, 1, 2, 4).reshape(rows, groups * width)


def pick_kernel(caption_ref, level_ref, table_ref, gate_ref, bias_ref, picked, sem):
    width = gate_ref.shape[1]
    seq_index = lax.axis_index("seq")
    sample = seq_index // SPAN
    level = level_ref[0, sample]
    first = pl.multiple_of(level // GATE_ROWS * GATE_ROWS, GATE_ROWS)
    start = pl.multiple_of(seq_index % SPAN * width, width)
    copy = pltpu.make_async_copy(
        table_ref.at[pl.ds(first, GATE_ROWS), pl.ds(start, width)], picked, sem
    )
    copy.start()
    slot = lax.broadcasted_iota(jnp.int32, bias_ref.shape, 0)
    bias_ref[...] = jnp.where(slot < caption_ref[0, sample], 0.0, -1e30)
    copy.wait()
    row = lax.broadcasted_iota(jnp.int32, (GATE_ROWS, 1), 0) == level - first
    gate_ref[...] = jnp.sum(
        jnp.where(row, picked[...].astype(jnp.float32), 0.0), axis=0, keepdims=True
    )


def pick(caption_len, noise_level, table, slots):
    width = table.shape[1] // SPAN
    return pl.pallas_call(
        pick_kernel,
        out_shape=(
            jax.ShapeDtypeStruct((1, width), jnp.float32),
            jax.ShapeDtypeStruct((slots, 1), jnp.float32),
        ),
        in_specs=[SMEM, SMEM, HBM],
        out_specs=(VMEM, VMEM),
        scratch_shapes=[pltpu.VMEM((GATE_ROWS, width), table.dtype), pltpu.SemaphoreType.DMA],
        compiler_params=PARAMS,
    )(caption_len, noise_level, pltpu.with_memory_space_constraint(table, pltpu.HBM))


def is_odd():
    return lax.axis_index("stretch") % 2 == 1


def part_of(ref, part, rows, cols):
    return ref[:, part * rows : (part + 1) * rows, cols].reshape(ref.shape[0] * rows, HD)


def scores(keys, query):
    return lax.dot_general(keys, query, NT, preferred_element_type=jnp.float32)


def weigh(weights, values):
    return lax.dot_general(
        weights.astype(jnp.bfloat16), values, TN, preferred_element_type=jnp.float32
    )


def key_top(scored):
    return jnp.max(scored, axis=0, keepdims=True)


def key_sum(weights):
    return jnp.sum(weights, axis=0, keepdims=True)


def heads_of(ref):
    return [slice(start, start + HD) for start in range(0, ref.shape[2], HD)]


def own_kernel(moved_ref, text_k_ref, text_v_ref, bias_ref, acc_ref, max_ref, total_ref):
    rows = moved_ref.shape[1] // 3
    heads = heads_of(moved_ref)
    scored = []
    for cols in heads:
        query = part_of(moved_ref, 0, rows, cols)
        own = scores(part_of(moved_ref, 1, rows, cols), query)
        scored.append((own, scores(text_k_ref[:, cols], query) + bias_ref[...]))
    weights = []
    for head, (own, text) in enumerate(scored):
        top = jnp.maximum(key_top(own), key_top(text))
        own = jnp.exp2((own - top) * SCALE)
        text = jnp.exp2((text - top) * SCALE)
        max_ref[head] = top
        total_ref[head] = key_sum(own) + key_sum(text)
        weights.append((own, text))
    for cols, (own, text) in zip(heads, weights):
        acc_ref[:, cols] = weigh(own, part_of(moved_ref, 2, rows, cols)) + weigh(
            text, text_v_ref[:, cols]
        )


def attend_own(moved, text_k, text_v, bias):
    rows = moved.shape[1] // 3 * SPAN
    width = moved.shape[2]
    stat = jax.ShapeDtypeStruct((width // HD, 1, rows), jnp.float32)
    return pl.pallas_call(
        own_kernel,
        out_shape=(jax.ShapeDtypeStruct((rows, width), jnp.float32), stat, stat),
        in_specs=[VMEM] * 4,
        out_specs=(VMEM,) * 3,
        compiler_params=PARAMS,
        cost_estimate=pl.CostEstimate(
            flops=336_000_000, bytes_accessed=1_500_000, transcendentals=655_360
        ),
    )(moved, text_k, text_v, bias)


def add_prior(moved_ref, prior_ref, has_prior, acc_ref, max_ref, total_ref, gate_ref, out_ref):
    rows = moved_ref.shape[1] // 3
    heads = heads_of(moved_ref)
    scored = [
        scores(part_of(prior_ref, 0, rows, cols), part_of(moved_ref, 0, rows, cols))
        for cols in heads
    ]
    weights = []
    for head, prior in enumerate(scored):
        own_top = max_ref[head]
        top = jnp.where(has_prior, jnp.maximum(own_top, key_top(prior)), own_top)
        shift = jnp.exp2((own_top - top) * SCALE)
        prior = jnp.exp2((prior - jnp.where(has_prior, top, 1e30)) * SCALE)
        total = total_ref[head] * shift + key_sum(prior)
        weights.append((prior, shift.reshape(-1, 1), total.reshape(-1, 1)))
    results = [
        weigh(prior, part_of(prior_ref, 1, rows, cols)) for cols, (prior, *_) in zip(heads, weights)
    ]
    for cols, result, (_, shift, total) in zip(heads, results, weights):
        attended = (acc_ref[:, cols] * shift + result) / total
        attended = attended.astype(jnp.bfloat16).astype(jnp.float32)
        gated = (gate_ref[:, cols] * attended).astype(out_ref.dtype)
        out_ref[:, :, cols] = gated.reshape(SPAN, rows, HD)


def even_kernel(moved_ref, far_ref, gate_ref, acc_ref, max_ref, total_ref, out_ref):
    @pl.when(jnp.logical_not(is_odd()))
    def _():
        has_prior = lax.axis_index("stretch") > 0
        add_prior(moved_ref, far_ref, has_prior, acc_ref, max_ref, total_ref, gate_ref, out_ref)


def odd_keys_kernel(moved_ref, keys_ref, max_ref, total_ref, weights_ref, shift_ref, sum_ref):
    @pl.when(is_odd())
    def _():
        rows = keys_ref.shape[1]
        scored = [
            scores(part_of(keys_ref, 0, rows, cols), part_of(moved_ref, 0, rows, cols))
            for cols in heads_of(keys_ref)
        ]
        for head, prior in enumerate(scored):
            own_top = max_ref[head]
            top = jnp.maximum(own_top, key_top(prior))
            shift = jnp.exp2((own_top - top) * SCALE)
            prior = jnp.exp2((prior - top) * SCALE)
            shift_ref[head] = shift
            sum_ref[head] = total_ref[head] * shift + key_sum(prior)
            weights_ref[head] = prior.astype(weights_ref.dtype)


def odd_keys(moved, keys, row_max, total):
    count, _, rows = total.shape
    stat = jax.ShapeDtypeStruct(total.shape, jnp.float32)
    return pl.pallas_call(
        odd_keys_kernel,
        out_shape=(jax.ShapeDtypeStruct((count, rows, rows), jnp.bfloat16), stat, stat),
        in_specs=[VMEM] * 4,
        out_specs=(VMEM,) * 3,
        compiler_params=PARAMS,
    )(moved, keys, row_max, total)


def odd_values_kernel(
    moved_ref, values_ref, weights_ref, acc_ref, shift_ref, sum_ref, gate_ref, even_ref, out_ref
):
    @pl.when(is_odd())
    def _():
        rows = values_ref.shape[1]
        heads = heads_of(values_ref)
        results = [
            weigh(weights_ref[head], part_of(values_ref, 0, rows, cols))
            for head, cols in enumerate(heads)
        ]
        for head, cols in enumerate(heads):
            shift, total = shift_ref[head].reshape(-1, 1), sum_ref[head].reshape(-1, 1)
            attended = (acc_ref[:, cols] * shift + results[head]) / total
            attended = attended.astype(jnp.bfloat16).astype(jnp.float32)
            gated = (gate_ref[:, cols] * attended).astype(out_ref.dtype)
            out_ref[:, :, cols] = gated.reshape(SPAN, rows, HD)

    @pl.when(jnp.logical_not(is_odd()))
    def _():
        out_ref[...] = even_ref[...]


def attend_last(kernel, *arrays, onto=None):
    moved = arrays[0]
    if onto is not None:
        arrays = (*arrays, onto)
    return pl.pallas_call(
        kernel,
        out_shape=jax.ShapeDtypeStruct(
            (SPAN, moved.shape[1] // 3, moved.shape[2]), jnp.bfloat16
        ),
        in_specs=[VMEM] * len(arrays),
        out_specs=VMEM,
        compiler_params=PARAMS,
        cost_estimate=pl.CostEstimate(
            flops=268_000_000, bytes_accessed=2_000_000, transcendentals=524_288
        ),
    )(*arrays)


def swap(blocks):
    videos = lax.axis_size("seq") // SPAN
    groups = [[video * SPAN + i for i in range(SPAN)] for video in range(videos)]
    return lax.all_to_all(blocks, "seq", 0, 0, axis_index_groups=groups)


def body(query, keys, values, text_keys, text_values, caption_len, noise_level, gate_table):
    tok_rows = query.shape[1]
    stretches = lax.axis_size("stretch")

    def exchanged():
        return swap(split(query[0], keys[0], values[0]))

    def shifted(blocks, first):
        route = [(i, i + 1) for i in range(first, stretches - 1, 2)]
        return lax.ppermute(blocks, "stretch", route)

    def rows_view(tiles):
        return rows_of(tiles).reshape(SPAN, 3 * tok_rows, -1)

    odd = is_odd()
    shape = jax.eval_shape(exchanged)
    early = lax.cond(odd, exchanged, lambda: jnp.zeros(shape.shape, shape.dtype))
    far = shifted(rows_view(early)[:, tok_rows:], 1)
    early, caption_len, noise_level = lax.optimization_barrier((early, caption_len, noise_level))
    gate, bias = pick(caption_len, noise_level, gate_table, text_keys.shape[2])
    odd, gate, bias = lax.optimization_barrier((odd, gate, bias))
    moved = rows_view(lax.cond(odd, lambda x: x, lambda x: exchanged(), early))
    near_keys = shifted(moved[:, tok_rows : 2 * tok_rows], 0)
    near_values = shifted(moved[:, 2 * tok_rows :], 0)
    text = (text_keys[0, 0], text_values[0, 0], bias)
    own = attend_own(moved, *text)
    mixed = attend_last(even_kernel, moved, far, gate, *own)
    acc, row_max, total = own
    weights, shift, total = odd_keys(moved, near_keys, row_max, total)
    mixed = attend_last(
        odd_values_kernel, moved, near_values, weights, acc, shift, total, gate, onto=mixed
    )
    return merge(swap(mixed))[None]


def solution(mesh):
    placed = (
        P("stretch", "seq", None),
        P("stretch", "seq", None),
        P("stretch", "seq", None),
        P("stretch", "seq", None, None),
        P("stretch", "seq", None, None),
        P("stretch", None),
        P("stretch", None),
        P(),
    )
    return jax.shard_map(
        body, mesh=mesh, in_specs=placed, out_specs=P("stretch", "seq", None), check_vma=False
    )
```

time: 53.5 us -> 52.7 us (0.985)
  the two profiles are of different devices: /device:TPU:1 before, /device:TPU:8 now
where the time goes in v4:
time: 52.7 us; the launch traced here: 52.4 us
  blocking collectives  42.5 us (81%)
  Pallas kernels  6.03 us (11%)
  starting transfers between devices  3.44 us (7%)
    all_to_all x2, blocking collectives, swap(): return lax.all_to_all(blocks, 'seq', 0, 0, axis_index_groups=groups)  42.5 us
    ppermute x3, starting transfers between devices, shifted(): return lax.ppermute(blocks, 'stretch', route)  3.44 us
    pallas_call x1, Pallas kernels, attend_own(): pl.pallas_call(own_kernel, out_shape=(jax.ShapeDtypeStruct((rows, width),...  1.36 us
    pallas_call x2, Pallas kernels, attend_last(): pl.pallas_call(kernel, out_shape=jax.ShapeDtypeStruct((SPAN, moved.shape[...  1.36 us
    pallas_call x1, Pallas kernels, pick(): pl.pallas_call(pick_kernel, out_shape=(jax.ShapeDtypeStruct((1, width), j...  1.29 us
    pallas_call x1, Pallas kernels, split(): pl.pallas_call(split_kernel, out_shape=jax.ShapeDtypeStruct((groups, len(...  1.26 us
  transfers between devices with their start and end apart: 3, of which 0 were waited for; matrix products, arithmetic and copies ran while one was open for 0% of the time, Pallas kernels for 10%

profile of v4, /device:TPU:8, one launch (start us, length us, event | category | flops | bytes accessed | tf_op | source)
XLA Modules:
  0.0 52.4 jit_solution(12816160774732893129)
XLA Ops:
  0.0 0.2 conditional.2
  0.0 0.2 broadcast.3
  0.2 0.0 copy-start
  0.2 0.0 copy-start.1
  0.3 0.7 %collective-permute-start.2 = (bf16[16,64,256]{2,1,0:T(8,128)(2,1)S(1)}, bf16[16,64,256]{2,1,0:T(8,128)(2,1)S(1)}, u32[]{:S(2)}, u32[]{:S(2)}) collective-permute-start(bf16[16,64,256]{2,1,0:T(8,128)(2,1)S(1)} %slice.14), channel_id=1, source_target_pairs={{64,128},{192,256},{320,384},{65,129},{193,257},{321,385},{66,130}... | collective-permute-start | bytes 1572872 | tf_op jit(solution)/shard_map/ppermute | solution.py:309
  1.0 0.0 copy-done
  1.0 0.0 copy-done.1
  1.0 1.3 %shard_map.82 = (f32[1,256]{1,0:T(1,128)S(1)}, f32[128,1]{1,0:T(8,128)S(1)}) custom-call(s32[1,4]{1,0:T(1,128)S(1)} %copy-done, s32[1,4]{1,0:T(1,128)S(1)} %copy-done.1, bf16[32,4096]{1,0:T(8,128)(2,1)} %table_ref.1), custom_call_target="tpu_custom_call" | custom-call | tf_op jit(solution)/shard_map/pallas_call | solution.py:110
  2.3 28.8 %conditional.3 = (bf16[16,3,4,2,8,128]{5,4,3,2,1,0:T(8,128)(2,1)S(1)}) conditional(s32[]{:T(128)} %convert_element_type.7, (bf16[1,32,4096]{2,1,0:T(8,128)(2,1)}, bf16[1,32,4096]{2,1,0:T(8,128)(2,1)}, bf16[1,32,4096]{2,1,0:T(8,128)(2,1)}) %tuple.20, bf16[16,3,4,2,8,128]{5,4,3,2,1,0:T(8,128)(2,1)S(1)} %get-tuple-element.60), branch_computations={%region_2.3_spmd, %region_3.4_spmd} | conditional | bytes 1572872 | solution.py:321
  2.3 1.3 %branch_0_fun.1 = bf16[16,3,4,2,8,128]{5,4,3,2,1,0:T(8,128)(2,1)S(1)} custom-call(bf16[4,16,2,8,128]{4,3,2,1,0:T(8,128)(2,1)} %bitcast.42, bf16[4,16,2,8,128]{4,3,2,1,0:T(8,128)(2,1)} %bitcast.44, bf16[4,16,2,8,128]{4,3,2,1,0:T(8,128)(2,1)} %bitcast.46), custom_call_target="tpu_custom_call" | custom-call | tf_op jit(solution)/shard_map/cond/branch_0_fun/pallas_call | solution.py:52
  3.6 27.5 %all_to_all.14 = bf16[16,3,4,2,8,128]{5,4,3,2,1,0:T(8,128)(2,1)S(1)} all-to-all(bf16[16,3,4,2,8,128]{5,4,3,2,1,0:T(8,128)(2,1)S(1)} %branch_0_fun.1), channel_id=1, replica_groups={{0,1,2,3,4,5,6,7,8,9,10,11,12,13,14,15},{16,17,18,19,20,21,22,23,24,25,..., dimensions={0} | all-to-all | bytes 1572864 | tf_op jit(solution)/shard_map/cond/branch_0_fun/all_to_all | solution.py:297
  31.1 0.0 copy-start.2
  31.1 0.0 copy-start.3
  31.1 1.4 %collective-permute-start.1 = (bf16[16,32,256]{2,1,0:T(8,128)(2,1)S(1)}, bf16[16,32,256]{2,1,0:T(8,128)(2,1)S(1)}, u32[]{:S(2)}, u32[]{:S(2)}) collective-permute-start(bf16[16,32,256]{2,1,0:T(8,128)(2,1)S(1)} %get-tuple-element.58), channel_id=1, source_target_pairs={{0,64},{128,192},{256,320},{384,448},{1,65},{129,193},{257,321},{3... | collective-permute-start | bytes 786440 | tf_op jit(solution)/shard_map/ppermute | solution.py:309
  32.6 1.3 %collective-permute-start = (bf16[16,32,256]{2,1,0:T(8,128)(2,1)S(1)}, bf16[16,32,256]{2,1,0:T(8,128)(2,1)S(1)}, u32[]{:S(2)}, u32[]{:S(2)}) collective-permute-start(bf16[16,32,256]{2,1,0:T(8,128)(2,1)S(1)} %get-tuple-element.59), channel_id=1, source_target_pairs={{0,64},{128,192},{256,320},{384,448},{1,65},{129,193},{257,321},{3... | collective-permute-start | bytes 786440 | tf_op jit(solution)/shard_map/ppermute | solution.py:309
  33.9 0.0 copy-done.2
  33.9 0.0 copy-done.3
  33.9 1.4 %shard_map.83 = (f32[512,256]{1,0:T(8,128)S(1)}, f32[2,1,512]{2,1,0:T(1,128)S(1)}, f32[2,1,512]{2,1,0:T(1,128)S(1)}) custom-call(bf16[16,96,256]{2,1,0:T(8,128)(2,1)S(1)} %bitcast.37, bf16[128,256]{1,0:T(8,128)(2,1)S(1)} %bitcast.33, bf16[128,256]{1,0:T(8,128)(2,1)S(1)} %bitcast.34, f32[128,1]{1,0:T(8,128)S(1)} %get-tuple-element.50.bias_ref), custom_call_target="tpu_custom_call" | custom-call | flops 336000000 | bytes 1500000 | tf_op jit(solution)/shard_map/pallas_call | solution.py:179
  35.3 0.0 collective-permute-done.1.keys_ref
  35.3 0.0 collective-permute-done.2.far_ref
  35.3 1.3 %shard_map.85.even_ref = bf16[16,32,256]{2,1,0:T(8,128)(2,1)S(1)} custom-call(bf16[16,96,256]{2,1,0:T(8,128)(2,1)S(1)} %bitcast.39, bf16[16,64,256]{2,1,0:T(8,128)(2,1)S(1)} %collective-permute-done.2.far_ref, f32[1,256]{1,0:T(1,128)S(1)} %get-tuple-element.57.gate_ref, f32[512,256]{1,0:T(8,128)S(1)} %get-tuple-element.54.acc_ref, ...), custom_call_target="tpu_custom_call" | custom-call | flops 268000000 | bytes 2000000 | tf_op jit(solution)/shard_map/pallas_call | solution.py:280
  36.7 0.0 collective-permute-done.values_ref
  36.7 15.0 %all_to_all.15 = bf16[16,32,256]{2,1,0:T(8,128)(2,1)S(1)} all-to-all(bf16[16,32,256]{2,1,0:T(8,128)(2,1)S(1)} %shard_map.86), channel_id=1, replica_groups={{0,1,2,3,4,5,6,7,8,9,10,11,12,13,14,15},{16,17,18,19,20,21,22,23,24,25,..., dimensions={0} | all-to-all | bytes 524288 | tf_op jit(solution)/shard_map/all_to_all | solution.py:297
  51.7 0.7 %shard_map.87 = bf16[4,16,2,8,128]{4,3,2,1,0:T(8,128)(2,1)} custom-call(bf16[16,4,2,8,128]{4,3,2,1,0:T(8,128)(2,1)S(1)} %bitcast.32), custom_call_target="tpu_custom_call" | custom-call | tf_op jit(solution)/shard_map/pallas_call | solution.py:77
  (4 shorter events, 0.1 us)
Async XLA Ops:
  0.2 0.8 %copy-start = (s32[1,4]{1,0:T(1,128)S(1)}, s32[1,4]{1,0:T(1,128)}, u32[]{:S(2)}) copy-start(s32[1,4]{1,0:T(1,128)} %caption_ref) | copy-start | bytes 52
  0.2 0.8 %copy-start.1 = (s32[1,4]{1,0:T(1,128)S(1)}, s32[1,4]{1,0:T(1,128)}, u32[]{:S(2)}) copy-start(s32[1,4]{1,0:T(1,128)} %level_ref) | copy-start | bytes 52
  0.3 35.1 %collective-permute-start.2 = (bf16[16,64,256]{2,1,0:T(8,128)(2,1)S(1)}, bf16[16,64,256]{2,1,0:T(8,128)(2,1)S(1)}, u32[]{:S(2)}, u32[]{:S(2)}) collective-permute-start(bf16[16,64,256]{2,1,0:T(8,128)(2,1)S(1)} %slice.14), channel_id=1, source_target_pairs={{64,128},{192,256},{320,384},{65,129},{193,257},{321,385},{66,130}... | collective-permute-start | bytes 1572872 | tf_op jit(solution)/shard_map/ppermute | solution.py:309
  31.1 2.8 %copy-start.2 = (bf16[1,1,128,256]{3,2,1,0:T(8,128)(2,1)S(1)}, bf16[1,1,128,256]{3,2,1,0:T(8,128)(2,1)}, u32[]{:S(2)}) copy-start(bf16[1,1,128,256]{3,2,1,0:T(8,128)(2,1)} %param.15) | copy-start | bytes 196612
  31.1 2.8 %copy-start.3 = (bf16[1,1,128,256]{3,2,1,0:T(8,128)(2,1)S(1)}, bf16[1,1,128,256]{3,2,1,0:T(8,128)(2,1)}, u32[]{:S(2)}) copy-start(bf16[1,1,128,256]{3,2,1,0:T(8,128)(2,1)} %param.16) | copy-start | bytes 196612
  31.1 4.1 %collective-permute-start.1 = (bf16[16,32,256]{2,1,0:T(8,128)(2,1)S(1)}, bf16[16,32,256]{2,1,0:T(8,128)(2,1)S(1)}, u32[]{:S(2)}, u32[]{:S(2)}) collective-permute-start(bf16[16,32,256]{2,1,0:T(8,128)(2,1)S(1)} %get-tuple-element.58), channel_id=1, source_target_pairs={{0,64},{128,192},{256,320},{384,448},{1,65},{129,193},{257,321},{3... | collective-permute-start | bytes 786440 | tf_op jit(solution)/shard_map/ppermute | solution.py:309
  32.6 4.1 %collective-permute-start = (bf16[16,32,256]{2,1,0:T(8,128)(2,1)S(1)}, bf16[16,32,256]{2,1,0:T(8,128)(2,1)S(1)}, u32[]{:S(2)}, u32[]{:S(2)}) collective-permute-start(bf16[16,32,256]{2,1,0:T(8,128)(2,1)S(1)} %get-tuple-element.59), channel_id=1, source_target_pairs={{0,64},{128,192},{256,320},{384,448},{1,65},{129,193},{257,321},{3... | collective-permute-start | bytes 786440 | tf_op jit(solution)/shard_map/ppermute | solution.py:309

commit v5 on v4

--- a/solution.py
+++ b/solution.py
@@ -85,39 +85,58 @@
     return out.transpose(0, 3, 1, 2, 4).reshape(rows, groups * width)
 
 
-def pick_kernel(caption_ref, level_ref, table_ref, gate_ref, bias_ref, picked, sem):
+def pick_kernel(
+    caption_ref, level_ref, table_ref, text_k_hbm, text_v_hbm,
+    gate_ref, bias_ref, text_k_ref, text_v_ref, picked, sems,
+):
     width = gate_ref.shape[1]
     seq_index = lax.axis_index("seq")
     sample = seq_index // SPAN
     level = level_ref[0, sample]
     first = pl.multiple_of(level // GATE_ROWS * GATE_ROWS, GATE_ROWS)
     start = pl.multiple_of(seq_index % SPAN * width, width)
-    copy = pltpu.make_async_copy(
-        table_ref.at[pl.ds(first, GATE_ROWS), pl.ds(start, width)], picked, sem
-    )
-    copy.start()
+    copies = [
+        pltpu.make_async_copy(
+            table_ref.at[pl.ds(first, GATE_ROWS), pl.ds(start, width)], picked, sems.at[0]
+        ),
+        pltpu.make_async_copy(text_k_hbm, text_k_ref, sems.at[1]),
+        pltpu.make_async_copy(text_v_hbm, text_v_ref, sems.at[2]),
+    ]
+    for copy in copies:
+        copy.start()
     slot = lax.broadcasted_iota(jnp.int32, bias_ref.shape, 0)
     bias_ref[...] = jnp.where(slot < caption_ref[0, sample], 0.0, -1e30)
-    copy.wait()
+    for copy in copies:
+        copy.wait()
     row = lax.broadcasted_iota(jnp.int32, (GATE_ROWS, 1), 0) == level - first
     gate_ref[...] = jnp.sum(
         jnp.where(row, picked[...].astype(jnp.float32), 0.0), axis=0, keepdims=True
     )
 
 
-def pick(caption_len, noise_level, table, slots):
+def pick(caption_len, noise_level, *arrays):
+    table, text_k, text_v = arrays
     width = table.shape[1] // SPAN
     return pl.pallas_call(
         pick_kernel,
         out_shape=(
             jax.ShapeDtypeStruct((1, width), jnp.float32),
-            jax.ShapeDtypeStruct((slots, 1), jnp.float32),
-        ),
-        in_specs=[SMEM, SMEM, HBM],
-        out_specs=(VMEM, VMEM),
-        scratch_shapes=[pltpu.VMEM((GATE_ROWS, width), table.dtype), pltpu.SemaphoreType.DMA],
-        compiler_params=PARAMS,
-    )(caption_len, noise_level, pltpu.with_memory_space_constraint(table, pltpu.HBM))
+            jax.ShapeDtypeStruct((text_k.shape[0], 1), jnp.float32),
+            jax.ShapeDtypeStruct(text_k.shape, text_k.dtype),
+            jax.ShapeDtypeStruct(text_v.shape, text_v.dtype),
+        ),
+        in_specs=[SMEM, SMEM] + [HBM] * 3,
+        out_specs=(VMEM,) * 4,
+        scratch_shapes=[
+            pltpu.VMEM((GATE_ROWS, width), table.dtype),
+            pltpu.SemaphoreType.DMA((3,)),
+        ],
+        compiler_params=PARAMS,
+    )(
+        caption_len,
+        noise_level,
+        *(pltpu.with_memory_space_constraint(array, pltpu.HBM) for array in arrays),
+    )
 
 
 def is_odd():
@@ -220,53 +239,12 @@
         add_prior(moved_ref, far_ref, has_prior, acc_ref, max_ref, total_ref, gate_ref, out_ref)
 
 
-def odd_keys_kernel(moved_ref, keys_ref, max_ref, total_ref, weights_ref, shift_ref, sum_ref):
-    @pl.when(is_odd())
-    def _():
-        rows = keys_ref.shape[1]
-        scored = [
-            scores(part_of(keys_ref, 0, rows, cols), part_of(moved_ref, 0, rows, cols))
-            for cols in heads_of(keys_ref)
-        ]
-        for head, prior in enumerate(scored):
-            own_top = max_ref[head]
-            top = jnp.maximum(own_top, key_top(prior))
-            shift = jnp.exp2((own_top - top) * SCALE)
-            prior = jnp.exp2((prior - top) * SCALE)
-            shift_ref[head] = shift
-            sum_ref[head] = total_ref[head] * shift + key_sum(prior)
-            weights_ref[head] = prior.astype(weights_ref.dtype)
-
-
-def odd_keys(moved, keys, row_max, total):
-    count, _, rows = total.shape
-    stat = jax.ShapeDtypeStruct(total.shape, jnp.float32)
-    return pl.pallas_call(
-        odd_keys_kernel,
-        out_shape=(jax.ShapeDtypeStruct((count, rows, rows), jnp.bfloat16), stat, stat),
-        in_specs=[VMEM] * 4,
-        out_specs=(VMEM,) * 3,
-        compiler_params=PARAMS,
-    )(moved, keys, row_max, total)
-
-
-def odd_values_kernel(
-    moved_ref, values_ref, weights_ref, acc_ref, shift_ref, sum_ref, gate_ref, even_ref, out_ref
+def odd_kernel(
+    moved_ref, near_ref, gate_ref, acc_ref, max_ref, total_ref, even_ref, out_ref
 ):
     @pl.when(is_odd())
     def _():
-        rows = values_ref.shape[1]
-        heads = heads_of(values_ref)
-        results = [
-            weigh(weights_ref[head], part_of(values_ref, 0, rows, cols))
-            for head, cols in enumerate(heads)
-        ]
-        for head, cols in enumerate(heads):
-            shift, total = shift_ref[head].reshape(-1, 1), sum_ref[head].reshape(-1, 1)
-            attended = (acc_ref[:, cols] * shift + results[head]) / total
-            attended = attended.astype(jnp.bfloat16).astype(jnp.float32)
-            gated = (gate_ref[:, cols] * attended).astype(out_ref.dtype)
-            out_ref[:, :, cols] = gated.reshape(SPAN, rows, HD)
+        add_prior(moved_ref, near_ref, True, acc_ref, max_ref, total_ref, gate_ref, out_ref)
 
     @pl.when(jnp.logical_not(is_odd()))
     def _():
@@ -316,19 +294,16 @@
     early = lax.cond(odd, exchanged, lambda: jnp.zeros(shape.shape, shape.dtype))
     far = shifted(rows_view(early)[:, tok_rows:], 1)
     early, caption_len, noise_level = lax.optimization_barrier((early, caption_len, noise_level))
-    gate, bias = pick(caption_len, noise_level, gate_table, text_keys.shape[2])
-    odd, gate, bias = lax.optimization_barrier((odd, gate, bias))
+    gate, bias, *text = pick(
+        caption_len, noise_level, gate_table, text_keys[0, 0], text_values[0, 0]
+    )
+    odd, gate, bias, *text = lax.optimization_barrier((odd, gate, bias, *text))
     moved = rows_view(lax.cond(odd, lambda x: x, lambda x: exchanged(), early))
-    near_keys = shifted(moved[:, tok_rows : 2 * tok_rows], 0)
-    near_values = shifted(moved[:, 2 * tok_rows :], 0)
-    text = (text_keys[0, 0], text_values[0, 0], bias)
+    near = shifted(moved[:, tok_rows:], 0)
+    text = (*text, bias)
     own = attend_own(moved, *text)
     mixed = attend_last(even_kernel, moved, far, gate, *own)
-    acc, row_max, total = own
-    weights, shift, total = odd_keys(moved, near_keys, row_max, total)
-    mixed = attend_last(
-        odd_values_kernel, moved, near_values, weights, acc, shift, total, gate, onto=mixed
-    )
+    mixed = attend_last(odd_kernel, moved, near, gate, *own, onto=mixed)
     return merge(swap(mixed))[None]
 
 

time: 52.7 us -> 52.6 us (level)
  the two profiles are of different devices: /device:TPU:8 before, /device:TPU:328 now
where the time goes in v5:
time: 52.6 us; the launch traced here: 52.3 us
  blocking collectives  41.3 us (79%)
  Pallas kernels  6.19 us (12%)
  starting transfers between devices  2.61 us (5%)
  waiting for transfers between devices  1.09 us (2%)
  local copies, waits for them, and re-layouts  0.9 us (2%)
    all_to_all x2, blocking collectives, swap(): return lax.all_to_all(blocks, 'seq', 0, 0, axis_index_groups=groups)  41.3 us
    ppermute x2, starting transfers between devices, shifted(): return lax.ppermute(blocks, 'stretch', route)  2.61 us
    pallas_call x1, Pallas kernels, pick(): pl.pallas_call(pick_kernel, out_shape=(jax.ShapeDtypeStruct((1, width), j...  1.49 us
    pallas_call x1, Pallas kernels, attend_own(): pl.pallas_call(own_kernel, out_shape=(jax.ShapeDtypeStruct((rows, width),...  1.37 us
    pallas_call x2, Pallas kernels, attend_last(): pl.pallas_call(kernel, out_shape=jax.ShapeDtypeStruct((SPAN, moved.shape[...  1.34 us
    pallas_call x1, Pallas kernels, split(): pl.pallas_call(split_kernel, out_shape=jax.ShapeDtypeStruct((groups, len(...  1.26 us
    ppermute x2, waiting for transfers between devices, shifted(): return lax.ppermute(blocks, 'stretch', route)  1.09 us
  transfers between devices with their start and end apart: 2, of which 1 were waited for; matrix products, arithmetic and copies ran while one was open for 0% of the time, Pallas kernels for 10%

profile of v5, /device:TPU:328, one launch (start us, length us, event | category | flops | bytes accessed | tf_op | source)
XLA Modules:
  0.0 52.3 jit_solution(10300687905833587365)
XLA Ops:
  0.0 0.2 conditional.2
  0.0 0.2 broadcast.3
  0.2 1.3 %collective-permute-start.1 = (bf16[16,64,256]{2,1,0:T(8,128)(2,1)S(1)}, bf16[16,64,256]{2,1,0:T(8,128)(2,1)S(1)}, u32[]{:S(2)}, u32[]{:S(2)}) collective-permute-start(bf16[16,64,256]{2,1,0:T(8,128)(2,1)S(1)} %slice.9), channel_id=1, source_target_pairs={{64,128},{192,256},{320,384},{65,129},{193,257},{321,385},{66,130}... | collective-permute-start | bytes 1572872 | tf_op jit(solution)/shard_map/ppermute | solution.py:287
  1.5 0.0 copy-start
  1.5 0.0 copy-start.1
  1.6 0.6 %copy-done = s32[1,4]{1,0:T(1,128)S(1)} copy-done((s32[1,4]{1,0:T(1,128)S(1)}, s32[1,4]{1,0:T(1,128)}, u32[]{:S(2)}) %copy-start) | copy-done | bytes 40
  2.2 0.0 copy-done.1
  2.2 1.5 %shard_map.82 = (f32[1,256]{1,0:T(1,128)S(1)}, f32[128,1]{1,0:T(8,128)S(1)}, bf16[128,256]{1,0:T(8,128)(2,1)S(1)}, bf16[128,256]{1,0:T(8,128)(2,1)S(1)}) custom-call(s32[1,4]{1,0:T(1,128)S(1)} %copy-done, s32[1,4]{1,0:T(1,128)S(1)} %copy-done.1, bf16[32,4096]{1,0:T(8,128)(2,1)} %table_ref.1, bf16[128,256]{1,0:T(8,128)(2,1)} %bitcast.44, ...), custom_call_target="tpu_custom_call" | custom-call | tf_op jit(solution)/shard_map/pallas_call | solution.py:120
  3.7 27.4 %conditional.3 = (bf16[16,3,4,2,8,128]{5,4,3,2,1,0:T(8,128)(2,1)S(1)}) conditional(s32[]{:T(128)} %convert_element_type.7, (bf16[1,32,4096]{2,1,0:T(8,128)(2,1)}, bf16[1,32,4096]{2,1,0:T(8,128)(2,1)}, bf16[1,32,4096]{2,1,0:T(8,128)(2,1)}) %tuple.20, bf16[16,3,4,2,8,128]{5,4,3,2,1,0:T(8,128)(2,1)S(1)} %get-tuple-element.60), branch_computations={%region_2.3_spmd, %region_3.4_spmd} | conditional | bytes 1572872 | solution.py:301
  3.7 1.3 %branch_0_fun.1 = bf16[16,3,4,2,8,128]{5,4,3,2,1,0:T(8,128)(2,1)S(1)} custom-call(bf16[4,16,2,8,128]{4,3,2,1,0:T(8,128)(2,1)} %bitcast.39, bf16[4,16,2,8,128]{4,3,2,1,0:T(8,128)(2,1)} %bitcast.41, bf16[4,16,2,8,128]{4,3,2,1,0:T(8,128)(2,1)} %bitcast.43), custom_call_target="tpu_custom_call" | custom-call | tf_op jit(solution)/shard_map/cond/branch_0_fun/pallas_call | solution.py:52
  5.0 26.1 %all_to_all.14 = bf16[16,3,4,2,8,128]{5,4,3,2,1,0:T(8,128)(2,1)S(1)} all-to-all(bf16[16,3,4,2,8,128]{5,4,3,2,1,0:T(8,128)(2,1)S(1)} %branch_0_fun.1), channel_id=1, replica_groups={{0,1,2,3,4,5,6,7,8,9,10,11,12,13,14,15},{16,17,18,19,20,21,22,23,24,25,..., dimensions={0} | all-to-all | bytes 1572864 | tf_op jit(solution)/shard_map/cond/branch_0_fun/all_to_all | solution.py:275
  31.1 1.3 %collective-permute-start = (bf16[16,64,256]{2,1,0:T(8,128)(2,1)S(1)}, bf16[16,64,256]{2,1,0:T(8,128)(2,1)S(1)}, u32[]{:S(2)}, u32[]{:S(2)}) collective-permute-start(bf16[16,64,256]{2,1,0:T(8,128)(2,1)S(1)} %slice.8), channel_id=1, source_target_pairs={{0,64},{128,192},{256,320},{384,448},{1,65},{129,193},{257,321},{3... | collective-permute-start | bytes 1572872 | tf_op jit(solution)/shard_map/ppermute | solution.py:287
  32.5 1.4 %shard_map.83 = (f32[512,256]{1,0:T(8,128)S(1)}, f32[2,1,512]{2,1,0:T(1,128)S(1)}, f32[2,1,512]{2,1,0:T(1,128)S(1)}) custom-call(bf16[16,96,256]{2,1,0:T(8,128)(2,1)S(1)} %bitcast.35, bf16[128,256]{1,0:T(8,128)(2,1)S(1)} %get-tuple-element.54.text_k_ref, bf16[128,256]{1,0:T(8,128)(2,1)S(1)} %get-tuple-element.55.text_v_ref, ...), custom_call_target="tpu_custom_call" | custom-call | flops 336000000 | bytes 1500000 | tf_op jit(solution)/shard_map/pallas_call | solution.py:198
  33.8 1.1 %collective-permute-done.1.far_ref = bf16[16,64,256]{2,1,0:T(8,128)(2,1)S(1)} collective-permute-done((bf16[16,64,256]{2,1,0:T(8,128)(2,1)S(1)}, bf16[16,64,256]{2,1,0:T(8,128)(2,1)S(1)}, u32[]{:S(2)}, u32[]{:S(2)}) %collective-permute-start.1) | collective-permute-done | bytes 524320 | tf_op jit(solution)/shard_map/ppermute | solution.py:287
  34.9 1.3 %shard_map.84.even_ref = bf16[16,32,256]{2,1,0:T(8,128)(2,1)S(1)} custom-call(bf16[16,96,256]{2,1,0:T(8,128)(2,1)S(1)} %bitcast.36, bf16[16,64,256]{2,1,0:T(8,128)(2,1)S(1)} %collective-permute-done.1.far_ref, f32[1,256]{1,0:T(1,128)S(1)} %get-tuple-element.53.gate_ref, f32[512,256]{1,0:T(8,128)S(1)} %get-tuple-element.57.acc_ref, ...), custom_call_target="tpu_custom_call" | custom-call | flops 268000000 | bytes 2000000 | tf_op jit(solution)/shard_map/pallas_call | solution.py:258
  36.2 0.0 collective-permute-done.near_ref
  36.3 15.2 %all_to_all.15 = bf16[16,32,256]{2,1,0:T(8,128)(2,1)S(1)} all-to-all(bf16[16,32,256]{2,1,0:T(8,128)(2,1)S(1)} %shard_map.85), channel_id=1, replica_groups={{0,1,2,3,4,5,6,7,8,9,10,11,12,13,14,15},{16,17,18,19,20,21,22,23,24,25,..., dimensions={0} | all-to-all | bytes 524288 | tf_op jit(solution)/shard_map/all_to_all | solution.py:275
  51.5 0.7 %shard_map.86 = bf16[4,16,2,8,128]{4,3,2,1,0:T(8,128)(2,1)} custom-call(bf16[16,4,2,8,128]{4,3,2,1,0:T(8,128)(2,1)S(1)} %bitcast.32), custom_call_target="tpu_custom_call" | custom-call | tf_op jit(solution)/shard_map/pallas_call | solution.py:77
  (3 shorter events, 0.1 us)
Async XLA Ops:
  0.2 34.7 %collective-permute-start.1 = (bf16[16,64,256]{2,1,0:T(8,128)(2,1)S(1)}, bf16[16,64,256]{2,1,0:T(8,128)(2,1)S(1)}, u32[]{:S(2)}, u32[]{:S(2)}) collective-permute-start(bf16[16,64,256]{2,1,0:T(8,128)(2,1)S(1)} %slice.9), channel_id=1, source_target_pairs={{64,128},{192,256},{320,384},{65,129},{193,257},{321,385},{66,130}... | collective-permute-start | bytes 1572872 | tf_op jit(solution)/shard_map/ppermute | solution.py:287
  1.5 0.7 %copy-start = (s32[1,4]{1,0:T(1,128)S(1)}, s32[1,4]{1,0:T(1,128)}, u32[]{:S(2)}) copy-start(s32[1,4]{1,0:T(1,128)} %caption_ref) | copy-start | bytes 52
  1.5 0.7 %copy-start.1 = (s32[1,4]{1,0:T(1,128)S(1)}, s32[1,4]{1,0:T(1,128)}, u32[]{:S(2)}) copy-start(s32[1,4]{1,0:T(1,128)} %level_ref) | copy-start | bytes 52
  31.1 5.1 %collective-permute-start = (bf16[16,64,256]{2,1,0:T(8,128)(2,1)S(1)}, bf16[16,64,256]{2,1,0:T(8,128)(2,1)S(1)}, u32[]{:S(2)}, u32[]{:S(2)}) collective-permute-start(bf16[16,64,256]{2,1,0:T(8,128)(2,1)S(1)} %slice.8), channel_id=1, source_target_pairs={{0,64},{128,192},{256,320},{384,448},{1,65},{129,193},{257,321},{3... | collective-permute-start | bytes 1572872 | tf_op jit(solution)/shard_map/ppermute | solution.py:287

commit v6 on v5

--- a/solution.py
+++ b/solution.py
@@ -89,7 +89,7 @@
     caption_ref, level_ref, table_ref, text_k_hbm, text_v_hbm,
     gate_ref, bias_ref, text_k_ref, text_v_ref, picked, sems,
 ):
-    width = gate_ref.shape[1]
+    width = picked.shape[1]
     seq_index = lax.axis_index("seq")
     sample = seq_index // SPAN
     level = level_ref[0, sample]
@@ -111,7 +111,7 @@
     row = lax.broadcasted_iota(jnp.int32, (GATE_ROWS, 1), 0) == level - first
     gate_ref[...] = jnp.sum(
         jnp.where(row, picked[...].astype(jnp.float32), 0.0), axis=0, keepdims=True
-    )
+    ).reshape(width, 1)
 
 
 def pick(caption_len, noise_level, *arrays):
@@ -120,7 +120,7 @@
     return pl.pallas_call(
         pick_kernel,
         out_shape=(
-            jax.ShapeDtypeStruct((1, width), jnp.float32),
+            jax.ShapeDtypeStruct((width, 1), jnp.float32),
             jax.ShapeDtypeStruct((text_k.shape[0], 1), jnp.float32),
             jax.ShapeDtypeStruct(text_k.shape, text_k.dtype),
             jax.ShapeDtypeStruct(text_v.shape, text_v.dtype),
@@ -153,7 +153,7 @@
 
 def weigh(weights, values):
     return lax.dot_general(
-        weights.astype(jnp.bfloat16), values, TN, preferred_element_type=jnp.float32
+        values, weights.astype(jnp.bfloat16), TN, preferred_element_type=jnp.float32
     )
 
 
@@ -186,7 +186,7 @@
         total_ref[head] = key_sum(own) + key_sum(text)
         weights.append((own, text))
     for cols, (own, text) in zip(heads, weights):
-        acc_ref[:, cols] = weigh(own, part_of(moved_ref, 2, rows, cols)) + weigh(
+        acc_ref[cols, :] = weigh(own, part_of(moved_ref, 2, rows, cols)) + weigh(
             text, text_v_ref[:, cols]
         )
 
@@ -197,7 +197,7 @@
     stat = jax.ShapeDtypeStruct((width // HD, 1, rows), jnp.float32)
     return pl.pallas_call(
         own_kernel,
-        out_shape=(jax.ShapeDtypeStruct((rows, width), jnp.float32), stat, stat),
+        out_shape=(jax.ShapeDtypeStruct((width, rows), jnp.float32), stat, stat),
         in_specs=[VMEM] * 4,
         out_specs=(VMEM,) * 3,
         compiler_params=PARAMS,
@@ -221,15 +221,15 @@
         shift = jnp.exp2((own_top - top) * SCALE)
         prior = jnp.exp2((prior - jnp.where(has_prior, top, 1e30)) * SCALE)
         total = total_ref[head] * shift + key_sum(prior)
-        weights.append((prior, shift.reshape(-1, 1), total.reshape(-1, 1)))
+        weights.append((prior, shift, 1.0 / total))
     results = [
         weigh(prior, part_of(prior_ref, 1, rows, cols)) for cols, (prior, *_) in zip(heads, weights)
     ]
-    for cols, result, (_, shift, total) in zip(heads, results, weights):
-        attended = (acc_ref[:, cols] * shift + result) / total
+    for cols, result, (_, shift, inverse) in zip(heads, results, weights):
+        attended = (acc_ref[cols, :] * shift + result) * inverse
         attended = attended.astype(jnp.bfloat16).astype(jnp.float32)
-        gated = (gate_ref[:, cols] * attended).astype(out_ref.dtype)
-        out_ref[:, :, cols] = gated.reshape(SPAN, rows, HD)
+        gated = (gate_ref[cols, :] * attended).astype(out_ref.dtype)
+        out_ref[:, :, cols] = gated.T.reshape(SPAN, rows, HD)
 
 
 def even_kernel(moved_ref, far_ref, gate_ref, acc_ref, max_ref, total_ref, out_ref):

time: 52.6 us -> 52.5 us (level)
  the two profiles are of different devices: /device:TPU:328 before, /device:TPU:1 now
where the time goes in v6:
time: 52.5 us; the launch traced here: 51.6 us
  blocking collectives  39.1 us (74%)
  Pallas kernels  5.94 us (11%)
  waiting for transfers between devices  3.01 us (6%)
  starting transfers between devices  2.61 us (5%)
  local copies, waits for them, and re-layouts  0.73 us (1%)
    all_to_all x2, blocking collectives, swap(): return lax.all_to_all(blocks, 'seq', 0, 0, axis_index_groups=groups)  39.1 us
    ppermute x2, waiting for transfers between devices, shifted(): return lax.ppermute(blocks, 'stretch', route)  3.01 us
    ppermute x2, starting transfers between devices, shifted(): return lax.ppermute(blocks, 'stretch', route)  2.61 us
    pallas_call x1, Pallas kernels, pick(): pl.pallas_call(pick_kernel, out_shape=(jax.ShapeDtypeStruct((width, 1), j...  1.59 us
    pallas_call x1, Pallas kernels, split(): pl.pallas_call(split_kernel, out_shape=jax.ShapeDtypeStruct((groups, len(...  1.26 us
    pallas_call x1, Pallas kernels, attend_own(): pl.pallas_call(own_kernel, out_shape=(jax.ShapeDtypeStruct((width, rows),...  1.2 us
    pallas_call x2, Pallas kernels, attend_last(): pl.pallas_call(kernel, out_shape=jax.ShapeDtypeStruct((SPAN, moved.shape[...  1.18 us
  transfers between devices with their start and end apart: 2, of which 2 were waited for; matrix products, arithmetic and copies ran while one was open for 0% of the time, Pallas kernels for 5%

profile of v6, /device:TPU:1, one launch (start us, length us, event | category | flops | bytes accessed | tf_op | source)
XLA Modules:
  0.0 51.6 jit_solution(15918387171839421247)
XLA Ops:
  0.0 25.6 %conditional.2 = (bf16[16,3,4,2,8,128]{5,4,3,2,1,0:T(8,128)(2,1)S(1)}) conditional(s32[]{:T(128)} %convert_element_type.6, () %tuple.19, (bf16[1,32,4096]{2,1,0:T(8,128)(2,1)}, bf16[1,32,4096]{2,1,0:T(8,128)(2,1)}, bf16[1,32,4096]{2,1,0:T(8,128)(2,1)}) %tuple.20), branch_computations={%region_0.1_spmd, %region_1.2_spmd} | conditional | bytes 1572872 | solution.py:294
  0.0 1.3 %branch_1_fun.1 = bf16[16,3,4,2,8,128]{5,4,3,2,1,0:T(8,128)(2,1)S(1)} custom-call(bf16[4,16,2,8,128]{4,3,2,1,0:T(8,128)(2,1)} %bitcast.38, bf16[4,16,2,8,128]{4,3,2,1,0:T(8,128)(2,1)} %bitcast.40, bf16[4,16,2,8,128]{4,3,2,1,0:T(8,128)(2,1)} %bitcast.42), custom_call_target="tpu_custom_call" | custom-call | tf_op jit(solution)/shard_map/cond/branch_1_fun/pallas_call | solution.py:52
  1.3 24.4 %all_to_all.13 = bf16[16,3,4,2,8,128]{5,4,3,2,1,0:T(8,128)(2,1)S(1)} all-to-all(bf16[16,3,4,2,8,128]{5,4,3,2,1,0:T(8,128)(2,1)S(1)} %branch_1_fun.1), channel_id=1, replica_groups={{0,1,2,3,4,5,6,7,8,9,10,11,12,13,14,15},{16,17,18,19,20,21,22,23,24,25,..., dimensions={0} | all-to-all | bytes 1572864 | tf_op jit(solution)/shard_map/cond/branch_1_fun/all_to_all | solution.py:275
  25.7 1.3 %collective-permute-start.1 = (bf16[16,64,256]{2,1,0:T(8,128)(2,1)S(1)}, bf16[16,64,256]{2,1,0:T(8,128)(2,1)S(1)}, u32[]{:S(2)}, u32[]{:S(2)}) collective-permute-start(bf16[16,64,256]{2,1,0:T(8,128)(2,1)S(1)} %slice.9), channel_id=1, source_target_pairs={{64,128},{192,256},{320,384},{65,129},{193,257},{321,385},{66,130}... | collective-permute-start | bytes 1572872 | tf_op jit(solution)/shard_map/ppermute | solution.py:287
  27.0 0.0 copy-start
  27.0 0.0 copy-start.1
  27.0 0.6 %copy-done = s32[1,4]{1,0:T(1,128)S(1)} copy-done((s32[1,4]{1,0:T(1,128)S(1)}, s32[1,4]{1,0:T(1,128)}, u32[]{:S(2)}) %copy-start) | copy-done | bytes 40
  27.7 0.0 copy-done.1
  27.7 1.6 %shard_map.82 = (f32[256,1]{1,0:T(8,128)S(1)}, f32[128,1]{1,0:T(8,128)S(1)}, bf16[128,256]{1,0:T(8,128)(2,1)S(1)}, bf16[128,256]{1,0:T(8,128)(2,1)S(1)}) custom-call(s32[1,4]{1,0:T(1,128)S(1)} %copy-done, s32[1,4]{1,0:T(1,128)S(1)} %copy-done.1, bf16[32,4096]{1,0:T(8,128)(2,1)} %table_ref.1, bf16[128,256]{1,0:T(8,128)(2,1)} %bitcast.44, ...), custom_call_target="tpu_custom_call" | custom-call | tf_op jit(solution)/shard_map/pallas_call | solution.py:120
  29.3 1.3 %collective-permute-start = (bf16[16,64,256]{2,1,0:T(8,128)(2,1)S(1)}, bf16[16,64,256]{2,1,0:T(8,128)(2,1)S(1)}, u32[]{:S(2)}, u32[]{:S(2)}) collective-permute-start(bf16[16,64,256]{2,1,0:T(8,128)(2,1)S(1)} %slice.8), channel_id=1, source_target_pairs={{0,64},{128,192},{256,320},{384,448},{1,65},{129,193},{257,321},{3... | collective-permute-start | bytes 1572872 | tf_op jit(solution)/shard_map/ppermute | solution.py:287
  30.6 1.2 %shard_map.83 = (f32[256,512]{1,0:T(8,128)S(1)}, f32[2,1,512]{2,1,0:T(1,128)S(1)}, f32[2,1,512]{2,1,0:T(1,128)S(1)}) custom-call(bf16[16,96,256]{2,1,0:T(8,128)(2,1)S(1)} %bitcast.35, bf16[128,256]{1,0:T(8,128)(2,1)S(1)} %get-tuple-element.54.text_k_ref, bf16[128,256]{1,0:T(8,128)(2,1)S(1)} %get-tuple-element.55.text_v_ref, ...), custom_call_target="tpu_custom_call" | custom-call | flops 336000000 | bytes 1500000 | tf_op jit(solution)/shard_map/pallas_call | solution.py:198
  31.8 1.2 %collective-permute-done.1.far_ref = bf16[16,64,256]{2,1,0:T(8,128)(2,1)S(1)} collective-permute-done((bf16[16,64,256]{2,1,0:T(8,128)(2,1)S(1)}, bf16[16,64,256]{2,1,0:T(8,128)(2,1)S(1)}, u32[]{:S(2)}, u32[]{:S(2)}) %collective-permute-start.1) | collective-permute-done | bytes 524320 | tf_op jit(solution)/shard_map/ppermute | solution.py:287
  33.1 1.8 %collective-permute-done.near_ref = bf16[16,64,256]{2,1,0:T(8,128)(2,1)S(1)} collective-permute-done((bf16[16,64,256]{2,1,0:T(8,128)(2,1)S(1)}, bf16[16,64,256]{2,1,0:T(8,128)(2,1)S(1)}, u32[]{:S(2)}, u32[]{:S(2)}) %collective-permute-start) | collective-permute-done | bytes 524320 | tf_op jit(solution)/shard_map/ppermute | solution.py:287
  34.9 1.2 %shard_map.85 = bf16[16,32,256]{2,1,0:T(8,128)(2,1)S(1)} custom-call(bf16[16,96,256]{2,1,0:T(8,128)(2,1)S(1)} %bitcast.37, bf16[16,64,256]{2,1,0:T(8,128)(2,1)S(1)} %collective-permute-done.near_ref, f32[256,1]{1,0:T(8,128)S(1)} %get-tuple-element.53.gate_ref, f32[256,512]{1,0:T(8,128)S(1)} %get-tuple-element.57.acc_ref, ...), custom_call_target="tpu_custom_call" | custom-call | flops 268000000 | bytes 2000000 | tf_op jit(solution)/shard_map/pallas_call | solution.py:258
  36.0 14.8 %all_to_all.15 = bf16[16,32,256]{2,1,0:T(8,128)(2,1)S(1)} all-to-all(bf16[16,32,256]{2,1,0:T(8,128)(2,1)S(1)} %shard_map.85), channel_id=1, replica_groups={{0,1,2,3,4,5,6,7,8,9,10,11,12,13,14,15},{16,17,18,19,20,21,22,23,24,25,..., dimensions={0} | all-to-all | bytes 524288 | tf_op jit(solution)/shard_map/all_to_all | solution.py:275
  50.8 0.7 %shard_map.86 = bf16[4,16,2,8,128]{4,3,2,1,0:T(8,128)(2,1)} custom-call(bf16[16,4,2,8,128]{4,3,2,1,0:T(8,128)(2,1)S(1)} %bitcast.32), custom_call_target="tpu_custom_call" | custom-call | tf_op jit(solution)/shard_map/pallas_call | solution.py:77
  (4 shorter events, 0.1 us)
Async XLA Ops:
  25.7 7.4 %collective-permute-start.1 = (bf16[16,64,256]{2,1,0:T(8,128)(2,1)S(1)}, bf16[16,64,256]{2,1,0:T(8,128)(2,1)S(1)}, u32[]{:S(2)}, u32[]{:S(2)}) collective-permute-start(bf16[16,64,256]{2,1,0:T(8,128)(2,1)S(1)} %slice.9), channel_id=1, source_target_pairs={{64,128},{192,256},{320,384},{65,129},{193,257},{321,385},{66,130}... | collective-permute-start | bytes 1572872 | tf_op jit(solution)/shard_map/ppermute | solution.py:287
  27.0 0.7 %copy-start = (s32[1,4]{1,0:T(1,128)S(1)}, s32[1,4]{1,0:T(1,128)}, u32[]{:S(2)}) copy-start(s32[1,4]{1,0:T(1,128)} %caption_ref) | copy-start | bytes 52
  27.0 0.7 %copy-start.1 = (s32[1,4]{1,0:T(1,128)S(1)}, s32[1,4]{1,0:T(1,128)}, u32[]{:S(2)}) copy-start(s32[1,4]{1,0:T(1,128)} %level_ref) | copy-start | bytes 52
  29.3 5.5 %collective-permute-start = (bf16[16,64,256]{2,1,0:T(8,128)(2,1)S(1)}, bf16[16,64,256]{2,1,0:T(8,128)(2,1)S(1)}, u32[]{:S(2)}, u32[]{:S(2)}) collective-permute-start(bf16[16,64,256]{2,1,0:T(8,128)(2,1)S(1)} %slice.8), channel_id=1, source_target_pairs={{0,64},{128,192},{256,320},{384,448},{1,65},{129,193},{257,321},{3... | collective-permute-start | bytes 1572872 | tf_op jit(solution)/shard_map/ppermute | solution.py:287

commit v7 on v6

--- a/solution.py
+++ b/solution.py
@@ -169,7 +169,13 @@
     return [slice(start, start + HD) for start in range(0, ref.shape[2], HD)]
 
 
-def own_kernel(moved_ref, text_k_ref, text_v_ref, bias_ref, acc_ref, max_ref, total_ref):
+def own_kernel(*refs):
+    @pl.when(is_odd())
+    def _():
+        attend_part(*refs)
+
+
+def attend_part(moved_ref, text_k_ref, text_v_ref, bias_ref, acc_ref, max_ref, total_ref):
     rows = moved_ref.shape[1] // 3
     heads = heads_of(moved_ref)
     scored = []
@@ -232,11 +238,39 @@
         out_ref[:, :, cols] = gated.T.reshape(SPAN, rows, HD)
 
 
-def even_kernel(moved_ref, far_ref, gate_ref, acc_ref, max_ref, total_ref, out_ref):
+def even_kernel(
+    moved_ref, far_ref, text_k_ref, text_v_ref, bias_ref, gate_ref, out_ref
+):
     @pl.when(jnp.logical_not(is_odd()))
     def _():
+        rows = moved_ref.shape[1] // 3
+        heads = heads_of(moved_ref)
         has_prior = lax.axis_index("stretch") > 0
-        add_prior(moved_ref, far_ref, has_prior, acc_ref, max_ref, total_ref, gate_ref, out_ref)
+        scored = []
+        for cols in heads:
+            query = part_of(moved_ref, 0, rows, cols)
+            own = scores(part_of(moved_ref, 1, rows, cols), query)
+            text = scores(text_k_ref[:, cols], query) + bias_ref[...]
+            scored.append((own, text, scores(part_of(far_ref, 0, rows, cols), query)))
+        weights = []
+        for own, text, prior in scored:
+            top = jnp.maximum(key_top(own), key_top(text))
+            top = jnp.where(has_prior, jnp.maximum(top, key_top(prior)), top)
+            own = jnp.exp2((own - top) * SCALE)
+            text = jnp.exp2((text - top) * SCALE)
+            prior = jnp.exp2((prior - jnp.where(has_prior, top, 1e30)) * SCALE)
+            total = key_sum(own) + key_sum(text) + key_sum(prior)
+            weights.append((own, text, prior, 1.0 / total))
+        results = [
+            weigh(own, part_of(moved_ref, 2, rows, cols))
+            + weigh(text, text_v_ref[:, cols])
+            + weigh(prior, part_of(far_ref, 1, rows, cols))
+            for cols, (own, text, prior, _) in zip(heads, weights)
+        ]
+        for cols, result, (*_, inverse) in zip(heads, results, weights):
+            attended = (result * inverse).astype(jnp.bfloat16).astype(jnp.float32)
+            gated = (gate_ref[cols, :] * attended).astype(out_ref.dtype)
+            out_ref[:, :, cols] = gated.T.reshape(SPAN, rows, HD)
 
 
 def odd_kernel(
@@ -302,7 +336,7 @@
     near = shifted(moved[:, tok_rows:], 0)
     text = (*text, bias)
     own = attend_own(moved, *text)
-    mixed = attend_last(even_kernel, moved, far, gate, *own)
+    mixed = attend_last(even_kernel, moved, far, *text, gate)
     mixed = attend_last(odd_kernel, moved, near, gate, *own, onto=mixed)
     return merge(swap(mixed))[None]
 

time: 52.5 us -> 52.8 us (level); the launches traced: 51.6 us -> 52.5 us
  blocking collectives: 39.1 us -> 40.1 us
    all_to_all x2, blocking collectives: 39.1 us -> 40.1 us  [swap(): return lax.all_to_all(blocks, 'seq', 0, 0, axis_index_groups=groups)]
where the time goes in v7:
time: 52.8 us; the launch traced here: 52.5 us
  blocking collectives  40.1 us (76%)
  Pallas kernels  5.95 us (11%)
  waiting for transfers between devices  3 us (6%)
  starting transfers between devices  2.61 us (5%)
  local copies, waits for them, and re-layouts  0.73 us (1%)
    all_to_all x2, blocking collectives, swap(): return lax.all_to_all(blocks, 'seq', 0, 0, axis_index_groups=groups)  40.1 us
    ppermute x2, waiting for transfers between devices, shifted(): return lax.ppermute(blocks, 'stretch', route)  3 us
    ppermute x2, starting transfers between devices, shifted(): return lax.ppermute(blocks, 'stretch', route)  2.61 us
    pallas_call x1, Pallas kernels, pick(): pl.pallas_call(pick_kernel, out_shape=(jax.ShapeDtypeStruct((width, 1), j...  1.59 us
    pallas_call x1, Pallas kernels, split(): pl.pallas_call(split_kernel, out_shape=jax.ShapeDtypeStruct((groups, len(...  1.26 us
    pallas_call x1, Pallas kernels, attend_own(): pl.pallas_call(own_kernel, out_shape=(jax.ShapeDtypeStruct((width, rows),...  1.21 us
    pallas_call x2, Pallas kernels, attend_last(): pl.pallas_call(kernel, out_shape=jax.ShapeDtypeStruct((SPAN, moved.shape[...  1.17 us
  transfers between devices with their start and end apart: 2, of which 2 were waited for; matrix products, arithmetic and copies ran while one was open for 0% of the time, Pallas kernels for 5%

profile of v7, /device:TPU:1, one launch (start us, length us, event | category | flops | bytes accessed | tf_op | source)
XLA Modules:
  0.0 52.5 jit_solution(9501179701726550179)
XLA Ops:
  0.0 25.6 %conditional.2 = (bf16[16,3,4,2,8,128]{5,4,3,2,1,0:T(8,128)(2,1)S(1)}) conditional(s32[]{:T(128)} %convert_element_type.6, () %tuple.19, (bf16[1,32,4096]{2,1,0:T(8,128)(2,1)}, bf16[1,32,4096]{2,1,0:T(8,128)(2,1)}, bf16[1,32,4096]{2,1,0:T(8,128)(2,1)}) %tuple.20), branch_computations={%region_0.1_spmd, %region_1.2_spmd} | conditional | bytes 1572872 | solution.py:328
  0.0 1.3 %branch_1_fun.1 = bf16[16,3,4,2,8,128]{5,4,3,2,1,0:T(8,128)(2,1)S(1)} custom-call(bf16[4,16,2,8,128]{4,3,2,1,0:T(8,128)(2,1)} %bitcast.38, bf16[4,16,2,8,128]{4,3,2,1,0:T(8,128)(2,1)} %bitcast.40, bf16[4,16,2,8,128]{4,3,2,1,0:T(8,128)(2,1)} %bitcast.42), custom_call_target="tpu_custom_call" | custom-call | tf_op jit(solution)/shard_map/cond/branch_1_fun/pallas_call | solution.py:52
  1.3 24.4 %all_to_all.13 = bf16[16,3,4,2,8,128]{5,4,3,2,1,0:T(8,128)(2,1)S(1)} all-to-all(bf16[16,3,4,2,8,128]{5,4,3,2,1,0:T(8,128)(2,1)S(1)} %branch_1_fun.1), channel_id=1, replica_groups={{0,1,2,3,4,5,6,7,8,9,10,11,12,13,14,15},{16,17,18,19,20,21,22,23,24,25,..., dimensions={0} | all-to-all | bytes 1572864 | tf_op jit(solution)/shard_map/cond/branch_1_fun/all_to_all | solution.py:309
  25.7 1.3 %collective-permute-start.1 = (bf16[16,64,256]{2,1,0:T(8,128)(2,1)S(1)}, bf16[16,64,256]{2,1,0:T(8,128)(2,1)S(1)}, u32[]{:S(2)}, u32[]{:S(2)}) collective-permute-start(bf16[16,64,256]{2,1,0:T(8,128)(2,1)S(1)} %slice.9), channel_id=1, source_target_pairs={{64,128},{192,256},{320,384},{65,129},{193,257},{321,385},{66,130}... | collective-permute-start | bytes 1572872 | tf_op jit(solution)/shard_map/ppermute | solution.py:321
  27.0 0.0 copy-start
  27.0 0.0 copy-start.1
  27.0 0.6 %copy-done = s32[1,4]{1,0:T(1,128)S(1)} copy-done((s32[1,4]{1,0:T(1,128)S(1)}, s32[1,4]{1,0:T(1,128)}, u32[]{:S(2)}) %copy-start) | copy-done | bytes 40
  27.7 0.0 copy-done.1
  27.7 1.6 %shard_map.82 = (f32[256,1]{1,0:T(8,128)S(1)}, f32[128,1]{1,0:T(8,128)S(1)}, bf16[128,256]{1,0:T(8,128)(2,1)S(1)}, bf16[128,256]{1,0:T(8,128)(2,1)S(1)}) custom-call(s32[1,4]{1,0:T(1,128)S(1)} %copy-done, s32[1,4]{1,0:T(1,128)S(1)} %copy-done.1, bf16[32,4096]{1,0:T(8,128)(2,1)} %table_ref.1, bf16[128,256]{1,0:T(8,128)(2,1)} %bitcast.44, ...), custom_call_target="tpu_custom_call" | custom-call | tf_op jit(solution)/shard_map/pallas_call | solution.py:120
  29.3 1.3 %collective-permute-start = (bf16[16,64,256]{2,1,0:T(8,128)(2,1)S(1)}, bf16[16,64,256]{2,1,0:T(8,128)(2,1)S(1)}, u32[]{:S(2)}, u32[]{:S(2)}) collective-permute-start(bf16[16,64,256]{2,1,0:T(8,128)(2,1)S(1)} %slice.8), channel_id=1, source_target_pairs={{0,64},{128,192},{256,320},{384,448},{1,65},{129,193},{257,321},{3... | collective-permute-start | bytes 1572872 | tf_op jit(solution)/shard_map/ppermute | solution.py:321
  30.6 1.2 %shard_map.83 = (f32[256,512]{1,0:T(8,128)S(1)}, f32[2,1,512]{2,1,0:T(1,128)S(1)}, f32[2,1,512]{2,1,0:T(1,128)S(1)}) custom-call(bf16[16,96,256]{2,1,0:T(8,128)(2,1)S(1)} %bitcast.35, bf16[128,256]{1,0:T(8,128)(2,1)S(1)} %get-tuple-element.54.refs_1_.text_k_ref, bf16[128,256]{1,0:T(8,128)(2,1)S(1)} %get-tuple-element.55.refs_2_.text_v_ref, ...), custom_call_target="tpu_custom_call" | custom-call | flops 336000000 | bytes 1500000 | tf_op jit(solution)/shard_map/pallas_call | solution.py:204
  31.9 1.2 %collective-permute-done.1.far_ref = bf16[16,64,256]{2,1,0:T(8,128)(2,1)S(1)} collective-permute-done((bf16[16,64,256]{2,1,0:T(8,128)(2,1)S(1)}, bf16[16,64,256]{2,1,0:T(8,128)(2,1)S(1)}, u32[]{:S(2)}, u32[]{:S(2)}) %collective-permute-start.1) | collective-permute-done | bytes 524320 | tf_op jit(solution)/shard_map/ppermute | solution.py:321
  33.1 1.8 %collective-permute-done.near_ref = bf16[16,64,256]{2,1,0:T(8,128)(2,1)S(1)} collective-permute-done((bf16[16,64,256]{2,1,0:T(8,128)(2,1)S(1)}, bf16[16,64,256]{2,1,0:T(8,128)(2,1)S(1)}, u32[]{:S(2)}, u32[]{:S(2)}) %collective-permute-start) | collective-permute-done | bytes 524320 | tf_op jit(solution)/shard_map/ppermute | solution.py:321
  34.9 1.2 %shard_map.85 = bf16[16,32,256]{2,1,0:T(8,128)(2,1)S(1)} custom-call(bf16[16,96,256]{2,1,0:T(8,128)(2,1)S(1)} %bitcast.37, bf16[16,64,256]{2,1,0:T(8,128)(2,1)S(1)} %collective-permute-done.near_ref, f32[256,1]{1,0:T(8,128)S(1)} %get-tuple-element.53.gate_ref, f32[256,512]{1,0:T(8,128)S(1)} %get-tuple-element.57.acc_ref, ...), custom_call_target="tpu_custom_call" | custom-call | flops 268000000 | bytes 2000000 | tf_op jit(solution)/shard_map/pallas_call | solution.py:292
  36.0 15.8 %all_to_all.15 = bf16[16,32,256]{2,1,0:T(8,128)(2,1)S(1)} all-to-all(bf16[16,32,256]{2,1,0:T(8,128)(2,1)S(1)} %shard_map.85), channel_id=1, replica_groups={{0,1,2,3,4,5,6,7,8,9,10,11,12,13,14,15},{16,17,18,19,20,21,22,23,24,25,..., dimensions={0} | all-to-all | bytes 524288 | tf_op jit(solution)/shard_map/all_to_all | solution.py:309
  51.8 0.7 %shard_map.86 = bf16[4,16,2,8,128]{4,3,2,1,0:T(8,128)(2,1)} custom-call(bf16[16,4,2,8,128]{4,3,2,1,0:T(8,128)(2,1)S(1)} %bitcast.32), custom_call_target="tpu_custom_call" | custom-call | tf_op jit(solution)/shard_map/pallas_call | solution.py:77
  (4 shorter events, 0.1 us)
Async XLA Ops:
  25.7 7.4 %collective-permute-start.1 = (bf16[16,64,256]{2,1,0:T(8,128)(2,1)S(1)}, bf16[16,64,256]{2,1,0:T(8,128)(2,1)S(1)}, u32[]{:S(2)}, u32[]{:S(2)}) collective-permute-start(bf16[16,64,256]{2,1,0:T(8,128)(2,1)S(1)} %slice.9), channel_id=1, source_target_pairs={{64,128},{192,256},{320,384},{65,129},{193,257},{321,385},{66,130}... | collective-permute-start | bytes 1572872 | tf_op jit(solution)/shard_map/ppermute | solution.py:321
  27.0 0.7 %copy-start = (s32[1,4]{1,0:T(1,128)S(1)}, s32[1,4]{1,0:T(1,128)}, u32[]{:S(2)}) copy-start(s32[1,4]{1,0:T(1,128)} %caption_ref) | copy-start | bytes 52
  27.0 0.7 %copy-start.1 = (s32[1,4]{1,0:T(1,128)S(1)}, s32[1,4]{1,0:T(1,128)}, u32[]{:S(2)}) copy-start(s32[1,4]{1,0:T(1,128)} %level_ref) | copy-start | bytes 52
  29.3 5.5 %collective-permute-start = (bf16[16,64,256]{2,1,0:T(8,128)(2,1)S(1)}, bf16[16,64,256]{2,1,0:T(8,128)(2,1)S(1)}, u32[]{:S(2)}, u32[]{:S(2)}) collective-permute-start(bf16[16,64,256]{2,1,0:T(8,128)(2,1)S(1)} %slice.8), channel_id=1, source_target_pairs={{0,64},{128,192},{256,320},{384,448},{1,65},{129,193},{257,321},{3... | collective-permute-start | bytes 1572872 | tf_op jit(solution)/shard_map/ppermute | solution.py:321
